TPU v7x, 1024 devices: a whole 8x8x8 slice. The times are simulated.
1024 devices in a mesh: dp: 16 (over y, core), expert: 64 (over z, x).
Axes of the slice: x: 8, y: 8, z: 8, core: 2. Of those that a mesh axis runs over, the one named last changes fastest.
Arguments:
- tokens: bfloat16 [1024, 7168], P('expert', 'dp'), may hold values from -6 to 6
- routes: int32 [1024, 8], P('expert'), may hold values from 0 to 31, all different within a row; in each aligned block of 16 rows (0 to 15, 16 to 31, ...) at most 8 rows name the same one
- probs: float32 [1024, 8], P('expert'), may hold values from 0.1 to 0.6
- cotangent: bfloat16 [1024, 7168], P('expert', 'dp'), may hold values from -6 to 6
- w_gate_up: bfloat16 [64, 7168, 2, 512], P('expert', 'dp'), may hold values from -0.0625 to 0.0625
- w_down: bfloat16 [64, 512, 7168], P('expert', None, 'dp'), may hold values from -0.1875 to 0.1875
Outputs:
- combined: bfloat16 [1024, 7168], P('expert', 'dp')
- d_tokens: bfloat16 [1024, 7168], P('expert', 'dp')
- grad_gate_up: bfloat16 [64, 7168, 2, 512], P('expert', 'dp')
Inputs may be any that keep to these rules, and one draw needn't show every extreme that they name: `routes`: each row names 8 different experts. Within each block of 16 rows (the tokens of one index of expert) no expert is named by more than 8 rows, a bound that some block reaches.
All inputs are finite; a program needn't handle non-finite values.
Results may differ from a plain program's by a relative error of at most 0.035.
Values may be sent and summed in bfloat16 or wider, within the bound.
A program may use at most 32 MiB of HBM per device.

v0:
```python
import jax
import jax.numpy as jnp
from jax import lax
from jax.sharding import PartitionSpec as P

CAP = 8


def gate_grads(d_hidden, gate_pre, up_pre):
    sigmoid_g = jax.nn.sigmoid(gate_pre)
    d_gate = d_hidden * up_pre * sigmoid_g * (1.0 + gate_pre * (1.0 - sigmoid_g))
    d_up = d_hidden * gate_pre * sigmoid_g
    return jnp.stack([d_gate, d_up], axis=1).astype(jnp.bfloat16)


def gated(pre_act):
    gate_pre = pre_act[:, 0]
    up_pre = pre_act[:, 1]
    return (gate_pre * jax.nn.sigmoid(gate_pre) * up_pre).astype(jnp.bfloat16)


def shards(tokens, routes, probs, cotangent, w_gate_up, w_down):
    tok_rows, span = tokens.shape
    fanout = routes.shape[1]
    experts_all = lax.axis_size("expert") // 2
    capacity = CAP
    flat_ids = routes.reshape(-1)
    onehot = (flat_ids[:, None] == jnp.arange(experts_all, dtype=jnp.int32)[None, :]).astype(
        jnp.int32
    )
    before = jnp.cumsum(onehot, axis=0) - onehot
    slot_rank = jnp.sum(before * onehot, axis=1)
    slot_index = flat_ids * capacity + slot_rank
    placer = (
        slot_index[None, :] == jnp.arange(experts_all * capacity, dtype=jnp.int32)[:, None]
    ).astype(jnp.bfloat16)
    x_routes = jnp.repeat(tokens, fanout, axis=0)
    cot_routes = (
        probs.reshape(-1)[:, None] * jnp.repeat(cotangent, fanout, axis=0).astype(jnp.float32)
    ).astype(jnp.bfloat16)
    send_x = jnp.dot(placer, x_routes, preferred_element_type=jnp.float32).astype(jnp.bfloat16)
    send_dy = jnp.dot(placer, cot_routes, preferred_element_type=jnp.float32).astype(jnp.bfloat16)
    send_x = jnp.repeat(send_x.reshape(experts_all, capacity, span), 2, axis=0)
    send_dy = jnp.repeat(send_dy.reshape(experts_all, capacity, span), 2, axis=0)
    recv_x, recv_dy = (
        lax.all_to_all(send_x, "expert", split_axis=0, concat_axis=0, tiled=True),
        lax.all_to_all(send_dy, "expert", split_axis=0, concat_axis=0, tiled=True),
    )
    rows_x = recv_x.reshape(-1, span)
    rows_dy = recv_dy.reshape(-1, span)
    w_gu = w_gate_up[0]
    w_dn = w_down[0]
    partial_value = jnp.einsum("rd,dgh->rgh", rows_x, w_gu, preferred_element_type=jnp.float32)
    d_partial_fn = lambda: lax.dot_general(
        rows_dy, w_dn, (((1,), (1,)), ((), ())), preferred_element_type=jnp.float32
    )
    pre_act = lax.psum(partial_value.astype(jnp.bfloat16), "dp").astype(jnp.float32)
    hidden = gated(pre_act)
    out_y = jnp.dot(hidden, w_dn, preferred_element_type=jnp.float32).astype(jnp.bfloat16)
    d_hidden = lax.psum(d_partial_fn().astype(jnp.bfloat16), "dp").astype(jnp.float32)
    d_pre = gate_grads(d_hidden, pre_act[:, 0], pre_act[:, 1])
    grad_w = jnp.einsum("rd,rgh->dgh", rows_x, d_pre, preferred_element_type=jnp.float32).astype(
        jnp.bfloat16
    )
    out_dx = jnp.einsum("rgh,dgh->rd", d_pre, w_gu, preferred_element_type=jnp.float32).astype(
        jnp.bfloat16
    )
    back_y, back_dx = (
        lax.all_to_all(
            out_y.reshape(-1, capacity, span), "expert", split_axis=0, concat_axis=0, tiled=True
        ),
        lax.all_to_all(
            out_dx.reshape(-1, capacity, span), "expert", split_axis=0, concat_axis=0, tiled=True
        ),
    )
    back_y = back_y.reshape(experts_all, 2, capacity, span)
    back_dx = back_dx.reshape(experts_all, 2, capacity, span)
    placer_t = placer.T
    route_y = jnp.dot(
        placer_t, back_y[:, 0].reshape(-1, span), preferred_element_type=jnp.float32
    ) + jnp.dot(placer_t, back_y[:, 1].reshape(-1, span), preferred_element_type=jnp.float32)
    route_dx = jnp.dot(
        placer_t, back_dx[:, 0].reshape(-1, span), preferred_element_type=jnp.float32
    ) + jnp.dot(placer_t, back_dx[:, 1].reshape(-1, span), preferred_element_type=jnp.float32)
    combined = jnp.sum(route_y.reshape(tok_rows, fanout, span) * probs[:, :, None], axis=1).astype(
        jnp.bfloat16
    )
    d_tokens = jnp.sum(route_dx.reshape(tok_rows, fanout, span), axis=1).astype(jnp.bfloat16)
    return (combined, d_tokens, grad_w[None])


def solution(mesh):
    placed = (
        P("expert", "dp"),
        P("expert", None),
        P("expert", None),
        P("expert", "dp"),
        P("expert", "dp", None, None),
        P("expert", None, "dp"),
    )
    return jax.shard_map(
        shards,
        mesh=mesh,
        in_specs=placed,
        out_specs=(P("expert", "dp"), P("expert", "dp"), P("expert", "dp", None, None)),
        check_vma=False,
    )
```

profile of v0, /device:TPU:1, one launch (start us, length us, event | category | flops | bytes accessed | tf_op | source)
XLA Modules:
  0.0 265.9 jit_solution(8880337555534605169)
XLA Ops:
  7.2 0.0 copy-start
  7.2 0.8 copy.24
  8.0 0.1 mul.64
  8.1 0.8 copy.16
  8.9 0.1 reshape.62
  9.0 0.7 convert_element_type.62
  9.7 0.1 fusion.36
  9.8 0.2 reduce_window_sum.11
  10.0 0.2 select_reduce_fusion
  10.1 0.3 convolution_convert_fusion.4
  10.5 0.1 copy.26
  10.6 0.0 copy-start.5
  10.7 0.8 broadcast_in_dim.22
  11.5 23.2 %all-to-all-start.2 = ((bf16[64,8,448]{2,1,0:T(8,128)(2,1)}), bf16[64,8,448]{2,1,0:T(8,128)(2,1)S(1)}, u32[]{:S(2)}, u32[]{:S(2)}) async-start(bf16[64,8,448]{2,1,0:T(8,128)(2,1)} %bitcast.15), calls=%async_computation.2 | async-start | bytes 1048576 | tf_op jit(solution)/shard_map/all_to_all | solution.py:47
  34.7 0.3 convolution_convert_fusion.5
  34.9 0.1 copy.17
  35.1 16.7 %all-to-all-done.2 = bf16[64,8,448]{2,1,0:T(8,128)(2,1)S(1)} async-done(((bf16[64,8,448]{2,1,0:T(8,128)(2,1)}), bf16[64,8,448]{2,1,0:T(8,128)(2,1)S(1)}, u32[]{:S(2)}, u32[]{:S(2)}) %all-to-all-start.2) | async-done | bytes 458784 | tf_op jit(solution)/shard_map/all_to_all | solution.py:47
  51.8 0.8 broadcast_in_dim.20
  52.7 6.8 %all-to-all-start = ((bf16[64,8,448]{2,1,0:T(8,128)(2,1)}), bf16[64,8,448]{2,1,0:T(8,128)(2,1)S(1)}, u32[]{:S(2)}, u32[]{:S(2)}) async-start(bf16[64,8,448]{2,1,0:T(8,128)(2,1)} %bitcast.2), calls=%async_computation | async-start | bytes 1048576 | tf_op jit(solution)/shard_map/all_to_all | solution.py:46
  59.4 0.0 all-reduce.3.cloned.1.call-start
  59.5 1.2 convolution_convert_fusion.2
  60.7 14.6 %all-to-all-done = bf16[64,8,448]{2,1,0:T(8,128)(2,1)S(1)} async-done(((bf16[64,8,448]{2,1,0:T(8,128)(2,1)}), bf16[64,8,448]{2,1,0:T(8,128)(2,1)S(1)}, u32[]{:S(2)}, u32[]{:S(2)}) %all-to-all-start) | async-done | bytes 458784 | tf_op jit(solution)/shard_map/all_to_all | solution.py:46
  75.4 0.0 copy-done
  75.4 1.7 convolution_convert_fusion
  77.1 0.0 all-reduce.3.cloned.1.call-update
  77.1 122.3 %all-reduce.3.cloned.1.call-done = (bf16[512,2,512]{2,0,1:T(8,128)(2,1)}, bf16[512,512]{1,0:T(8,128)(2,1)}) async-done(((bf16[512,2,512]{2,0,1:T(8,128)(2,1)}, bf16[512,512]{1,0:T(8,128)(2,1)}), (bf16[512,2,512]{2,0,1:T(8,128)(2,1)}, bf16[512,512]{1,0:T(8,128)(2,1)})) %all-reduce.3.cloned.1.call-update) | async-done | bytes 1572880 | tf_op jit(solution)/shard_map/psum | solution.py:57
  199.4 1.5 convert_element_type.57
  201.0 1.3 convolution_convert_fusion.3
  202.3 2.0 copy.20
  204.3 13.7 %all-to-all-start.1 = ((bf16[64,8,448]{2,1,0:T(8,128)(2,1)}), bf16[64,8,448]{2,1,0:T(8,128)(2,1)S(1)}, u32[]{:S(2)}, u32[]{:S(2)}) async-start(bf16[64,8,448]{2,1,0:T(8,128)(2,1)} %bitcast.104), calls=%async_computation.1 | async-start | bytes 1048576 | tf_op jit(solution)/shard_map/all_to_all | solution.py:69
  218.0 1.5 fusion.18
  219.5 0.0 copy-start.1
  219.5 0.8 copy-done.1
  220.3 0.2 copy-done.2
  220.5 0.7 fusion.1
  221.2 1.0 copy.28
  222.2 12.5 %all-to-all-done.1 = bf16[64,8,448]{2,1,0:T(8,128)(2,1)S(1)} async-done(((bf16[64,8,448]{2,1,0:T(8,128)(2,1)}), bf16[64,8,448]{2,1,0:T(8,128)(2,1)S(1)}, u32[]{:S(2)}, u32[]{:S(2)}) %all-to-all-start.1) | async-done | bytes 458784 | tf_op jit(solution)/shard_map/all_to_all | solution.py:69
  234.7 7.0 %all-to-all-start.3 = ((bf16[64,8,448]{2,1,0:T(8,128)(2,1)}), bf16[64,8,448]{2,1,0:T(8,128)(2,1)S(1)}, u32[]{:S(2)}, u32[]{:S(2)}) async-start(bf16[64,8,448]{2,1,0:T(8,128)(2,1)} %bitcast.22), calls=%async_computation.3 | async-start | bytes 1048576 | tf_op jit(solution)/shard_map/all_to_all | solution.py:72
  241.7 1.9 fusion
  243.6 1.9 copy.33
  245.4 0.3 fusion.22
  245.7 0.3 convolution_add_fusion.1
  246.0 0.1 copy.23
  246.1 11.4 %all-to-all-done.3 = bf16[64,8,448]{2,1,0:T(8,128)(2,1)S(1)} async-done(((bf16[64,8,448]{2,1,0:T(8,128)(2,1)}), bf16[64,8,448]{2,1,0:T(8,128)(2,1)S(1)}, u32[]{:S(2)}, u32[]{:S(2)}) %all-to-all-start.3) | async-done | bytes 458784 | tf_op jit(solution)/shard_map/all_to_all | solution.py:72
  257.5 0.3 fusion.21
  257.8 0.3 convolution_add_fusion
  258.1 0.1 copy.31
  258.2 0.8 bitcast_reduce_fusion
  (11 shorter events, 0.0 us)
Async XLA Ops:
  7.2 68.2 %copy-start = (bf16[1,448,2,512]{3,2,1,0:T(2,128)(2,1)S(1)}, bf16[1,448,2,512]{3,2,1,0:T(2,128)(2,1)}, u32[]{:S(2)}) copy-start(bf16[1,448,2,512]{3,2,1,0:T(2,128)(2,1)} %param.10) | copy-start | bytes 2752516
  7.2 27.5 %copy-start.7 = (bf16[16,448]{1,0:T(8,128)(2,1)S(1)}, bf16[16,448]{1,0:T(8,128)(2,1)}, u32[]{:S(2)}) copy-start(bf16[16,448]{1,0:T(8,128)(2,1)} %param.6) | copy-start | bytes 43012
  10.6 48.8 %copy-start.5 = (bf16[1,512,448]{1,2,0:T(8,128)(2,1)S(1)}, bf16[1,512,448]{1,2,0:T(8,128)(2,1)}, u32[]{:S(2)}) copy-start(bf16[1,512,448]{1,2,0:T(8,128)(2,1)} %param.11) | copy-start | bytes 1376260
  11.5 40.3 %all-to-all-start.2 = ((bf16[64,8,448]{2,1,0:T(8,128)(2,1)}), bf16[64,8,448]{2,1,0:T(8,128)(2,1)S(1)}, u32[]{:S(2)}, u32[]{:S(2)}) async-start(bf16[64,8,448]{2,1,0:T(8,128)(2,1)} %bitcast.15), calls=%async_computation.2 | async-start | bytes 1048576 | tf_op jit(solution)/shard_map/all_to_all | solution.py:47
  52.7 22.7 %all-to-all-start = ((bf16[64,8,448]{2,1,0:T(8,128)(2,1)}), bf16[64,8,448]{2,1,0:T(8,128)(2,1)S(1)}, u32[]{:S(2)}, u32[]{:S(2)}) async-start(bf16[64,8,448]{2,1,0:T(8,128)(2,1)} %bitcast.2), calls=%async_computation | async-start | bytes 1048576 | tf_op jit(solution)/shard_map/all_to_all | solution.py:46
  59.4 140.0 %all-reduce.3.cloned.1.call-start = ((), (), s32[]{:S(2)}) async-start(), calls=%async_computation.4 | async-start | bytes 3145728 | tf_op jit(solution)/shard_map/psum | solution.py:57
  75.4 1.8 copy-start.3
  77.1 123.9 %copy-start.6 = (bf16[1,512,448]{1,2,0:T(8,128)(2,1)S(1)}, bf16[1,512,448]{1,2,0:T(8,128)(2,1)}, u32[]{:S(2)}) copy-start(bf16[1,512,448]{1,2,0:T(8,128)(2,1)} %param.11) | copy-start | bytes 1376260
  204.3 30.4 %all-to-all-start.1 = ((bf16[64,8,448]{2,1,0:T(8,128)(2,1)}), bf16[64,8,448]{2,1,0:T(8,128)(2,1)S(1)}, u32[]{:S(2)}, u32[]{:S(2)}) async-start(bf16[64,8,448]{2,1,0:T(8,128)(2,1)} %bitcast.104), calls=%async_computation.1 | async-start | bytes 1048576 | tf_op jit(solution)/shard_map/all_to_all | solution.py:69
  219.5 0.8 copy-start.1
  219.5 1.0 copy-start.2
  220.5 21.2 %copy-start.4 = (bf16[64,8,448]{2,1,0:T(8,128)(2,1)S(1)}, bf16[64,8,448]{2,1,0:T(8,128)(2,1)}, u32[]{:S(2)}) copy-start(bf16[64,8,448]{2,1,0:T(8,128)(2,1)} %copy-done.3) | copy-start | bytes 1376260
  234.7 22.8 %all-to-all-start.3 = ((bf16[64,8,448]{2,1,0:T(8,128)(2,1)}), bf16[64,8,448]{2,1,0:T(8,128)(2,1)S(1)}, u32[]{:S(2)}, u32[]{:S(2)}) async-start(bf16[64,8,448]{2,1,0:T(8,128)(2,1)} %bitcast.22), calls=%async_computation.3 | async-start | bytes 1048576 | tf_op jit(solution)/shard_map/all_to_all | solution.py:72
Sparse Core Ops, SparseCore 0:
  77.2 122.1 all-reduce.2
where the time goes:
time: 271 us; the launch traced here: 266 us
  waiting for transfers between devices  178 us (66%)
  starting transfers between devices  50.6 us (19%)
  between operations  14.3 us (5%)
  local copies, waits for them, and re-layouts  9.86 us (4%)
  matrix products  8.54 us (3%)
  other arithmetic  5.02 us (2%)
    psum x1, waiting for transfers between devices, shards(): lax.psum(partial_value.astype(jnp.bfloat16), 'dp').astype(jnp.float32)  122 us
    all_to_all x1, starting transfers between devices, shards(): lax.all_to_all(send_dy, 'expert', split_axis=0, concat_axis=0, tiled=True)  23.2 us
    all_to_all x1, waiting for transfers between devices, shards(): lax.all_to_all(send_dy, 'expert', split_axis=0, concat_axis=0, tiled=True)  16.7 us
    all_to_all x1, waiting for transfers between devices, shards(): lax.all_to_all(send_x, 'expert', split_axis=0, concat_axis=0, tiled=True)  14.6 us
    all_to_all x1, starting transfers between devices, shards(): lax.all_to_all(out_y.reshape(-1, capacity, span), 'expert', split_axis=0,...  13.7 us
    all_to_all x1, waiting for transfers between devices, shards(): lax.all_to_all(out_y.reshape(-1, capacity, span), 'expert', split_axis=0,...  12.5 us
    all_to_all x1, waiting for transfers between devices, shards(): lax.all_to_all(out_dx.reshape(-1, capacity, span), 'expert', split_axis=0...  11.4 us
    all_to_all x1, starting transfers between devices, shards(): lax.all_to_all(out_dx.reshape(-1, capacity, span), 'expert', split_axis=0...  6.97 us
  transfers between devices with their start and end apart: 5, of which 5 were waited for; matrix products, arithmetic and copies ran while one was open for 3% of the time, Pallas kernels for 0%

commit v1 on v0

v1 whole, which is shorter than its diff:
```python
import functools

import jax
import jax.numpy as jnp
from jax import lax
from jax.experimental import pallas as pl
from jax.experimental.pallas import tpu as pltpu
from jax.sharding import PartitionSpec as P

CAP = 8
NX = 8
NZ = 8
NY = 8
BF = jnp.bfloat16
F32 = jnp.float32
MESH = pl.DeviceIdType.MESH
ORDER = (4, 3, 5, 2, 6, 1, 7)


def iota(shape, dim):
    return lax.broadcasted_iota(jnp.int32, shape, dim)


def dot(a, b):
    return jnp.dot(a, b, preferred_element_type=F32)


def dot_nt(a, b):
    return lax.dot_general(a, b, (((1,), (1,)), ((), ())), preferred_element_type=F32)


def dot_tn(a, b):
    return lax.dot_general(a, b, (((0,), (0,)), ((), ())), preferred_element_type=F32)


def rank_table(meta, rows_of):
    n = meta.shape[0]
    mask = (meta > 0).astype(F32)
    i, j = iota((n, n), 0), iota((n, n), 1)
    lower = ((i // rows_of == j // rows_of) & (j < i)).astype(F32).astype(BF)
    rank = dot(lower, mask.astype(BF))
    return jnp.where(mask > 0, rank, -1.0).astype(BF)


def place_table(table, expert_of, blocks, rows_of):
    n = table.shape[0]
    per = blocks * CAP
    width = expert_of.shape[1]
    select = (iota((128, width), 0) == 64 + expert_of).astype(F32).astype(BF)
    rank = dot(table, select)
    col = iota((n, width), 1) % per
    row = iota((n, width), 0) // rows_of
    return ((rank == (col % CAP).astype(F32)) & (col // CAP == row)).astype(F32).astype(BF)


def kernel(
    tok, cot, routes, probs, wgu, wdn, comb_o, dtok_o, grad_o,
    s1z, s1x, c1x, a1z, a1x, b1z, b1x, g1, g2, q1, q2, d1, d2, perm, x2, xr, xt, cr, prow,
    pa, sb, rb, pb, pr, da, tb, ub, vb, vr, pre, hg, dg, y2, o1, o2, e1, e2, f1, f2, k1, k2,
    ss_a, rs_a, ss_d, rs_d, ss_c, rs_c, ss_p, rs_p, ss_g, rs_g, ss_w, rs_w, ss_e, rs_e, ss_k, rs_k,
):
    nx, nz, ny = NX, NZ, NY
    dp, ex = lax.axis_index("dp"), lax.axis_index("expert")
    y, c = dp // 2, dp % 2
    z, x = ex // nx, ex % nx
    rows_of, span = tok.shape
    tail = span - 256
    rows = nz * nx * CAP
    half = rows // 2
    piece = half // ny
    hid = wdn.shape[0]
    tile = min(128, half)
    nbx, nbz = [d for d in ORDER if d < nx], [d for d in ORDER if d < nz]
    nby = [d for d in ORDER if d < ny]

    def at(y_=None, c_=None, z_=None, x_=None):
        return (
            (y if y_ is None else y_) * 2 + (c if c_ is None else c_),
            (z if z_ is None else z_) * nx + (x if x_ is None else x_),
        )

    def remote(src, dst, ss, rs, dev):
        return pltpu.make_async_remote_copy(
            src_ref=src, dst_ref=dst, send_sem=ss, recv_sem=rs, device_id=dev, device_id_type=MESH
        )

    def send_x(src, dst, ss, rs):
        for d in nbx:
            p = (x + d) % nx
            remote(src(p), dst.at[x], ss.at[p], rs.at[x], at(x_=p)).start()

    def send_z(src, dst, ss, rs):
        for d in nbz:
            p = (z + d) % nz
            remote(src(p), dst.at[z], ss.at[p], rs.at[z], at(z_=p)).start()

    def send_y(src, dst, ss, rs):
        for d in nby:
            p = (y + d) % ny
            remote(src(p), dst, ss.at[p], rs.at[y], at(y_=p)).start()

    def got(dst, rs, me, others, n):
        for d in others[::-1]:
            p = (me + d) % n
            remote(dst(p), dst(p), rs.at[p], rs.at[p], at()).wait_recv()

    def sent(src, ss, me, others, n):
        for d in others:
            p = (me + d) % n
            remote(src(p), src(p), ss.at[p], ss.at[p], at()).wait_send()

    barrier = pltpu.get_barrier_semaphore()
    for d in nbx:
        pl.semaphore_signal(barrier, 1, device_id=at(x_=(x + d) % nx), device_id_type=MESH)
    for d in nbz:
        pl.semaphore_signal(barrier, 1, device_id=at(z_=(z + d) % nz), device_id_type=MESH)
    for d in nby:
        pl.semaphore_signal(barrier, 1, device_id=at(y_=(y + d) % ny), device_id_type=MESH)
    pl.semaphore_signal(barrier, 1, device_id=at(c_=1 - c), device_id_type=MESH)

    lane = iota((rows_of, 128), 1)
    weight = jnp.zeros((rows_of, 128), F32)
    for k in range(routes.shape[1]):
        weight += jnp.where(routes[:, k : k + 1] == lane % 32, probs[:, k : k + 1], 0.0)
    high = weight.astype(BF).astype(F32)
    meta = jnp.where(lane < 64, 0.0, jnp.where(lane < 96, high, weight - high))
    s1z[:, 0:256] = tok[:, 0:256]
    s1z[:, 256:384] = meta.astype(BF)
    s1x[...] = jnp.zeros_like(s1x)
    s1x[:, 0:tail] = tok[:, 256:span]
    s1x[:, 128:256] = (s1x[:, 128:256].astype(F32) + meta).astype(BF)
    c1x[...] = jnp.zeros_like(c1x)
    c1x[:, 0:tail] = cot[:, 256:span]
    pl.semaphore_wait(barrier, len(nbx) + len(nbz) + len(nby) + 1)

    send_z(lambda p: s1z, a1z, ss_a.at[0], rs_a.at[0])
    send_x(lambda p: s1x, a1x, ss_a.at[1], rs_a.at[1])
    send_z(lambda p: cot.at[:, 0:256], b1z, ss_a.at[2], rs_a.at[2])
    send_x(lambda p: c1x, b1x, ss_a.at[3], rs_a.at[3])
    a1z[z] = s1z[...]
    a1x[x] = s1x[...]
    b1z[z] = cot[:, 0:256]
    b1x[x] = c1x[...]
    r_, c_ = iota((rows, rows), 0), iota((rows, rows), 1)
    perm[...] = (
        (r_ // CAP // nz == c_ // CAP % nx) & (r_ // CAP % nz == c_ // CAP // nx) & (r_ % CAP == c_ % CAP)
    ).astype(F32).astype(BF)

    wide = (1, nx * nz * CAP)
    got(lambda p: a1z.at[p], rs_a.at[0], z, nbz, nz)
    block = a1z[...].reshape(nz * rows_of, 384)
    table = rank_table(block[:, 256:384].astype(F32), rows_of)
    g1[...] = place_table(table, z * (nx // 2) + iota(wide, 1) // (nz * CAP) // 2, nz, rows_of)
    q1[0] = dot_tn(g1[...], block[:, 0:256]).astype(BF).reshape(nx, nz * CAP, 256)
    send_x(lambda p: q1.at[0, p], d1.at[0], ss_d.at[0], rs_d.at[0])
    got(lambda p: a1x.at[p], rs_a.at[1], x, nbx, nx)
    block = a1x[...].reshape(nx * rows_of, 256)
    table = rank_table(block[:, 128:256].astype(F32) * (iota((nx * rows_of, 128), 1) >= 64), rows_of)
    g2[...] = place_table(table, iota(wide, 1) // (nx * CAP) * (nx // 2) + x // 2, nx, rows_of)
    q2[0] = dot_tn(g2[...], block).astype(BF).reshape(nz, nx * CAP, 256)
    send_z(lambda p: q2.at[0, p], d2.at[0], ss_d.at[1], rs_d.at[1])
    got(lambda p: b1z.at[p], rs_a.at[2], z, nbz, nz)
    q1[1] = dot_tn(g1[...], b1z[...].reshape(nz * rows_of, 256)).astype(BF).reshape(nx, nz * CAP, 256)
    send_x(lambda p: q1.at[1, p], d1.at[1], ss_d.at[2], rs_d.at[2])
    got(lambda p: b1x.at[p], rs_a.at[3], x, nbx, nx)
    q2[1] = dot_tn(g2[...], b1x[...].reshape(nx * rows_of, 256)).astype(BF).reshape(nz, nx * CAP, 256)
    send_z(lambda p: q2.at[1, p], d2.at[1], ss_d.at[3], rs_d.at[3])
    d1[0, x] = q1[0, x]
    d2[0, z] = q2[0, z]
    d1[1, x] = q1[1, x]
    d2[1, z] = q2[1, z]

    def sweep(n, body):
        def step(i, _):
            body(pl.ds(pl.multiple_of(i * tile, tile), tile), i * tile)
            return 0

        lax.fori_loop(0, n // tile, step, 0)

    got(lambda p: d1.at[0, p], rs_d.at[0], x, nbx, nx)
    got(lambda p: d2.at[0, p], rs_d.at[1], z, nbz, nz)
    expert = z * (nx // 2) + x // 2
    x2[...] = d2[0].reshape(rows, 256)

    def arrange(at_, _):
        lower = dot(perm[at_, :], x2[...])
        gate = lower[:, 128:256]
        which = iota((tile, 128), 1)
        gate = jnp.where((which == 64 + expert) | (which == 96 + expert), gate, 0.0)
        prow[at_, :] = jnp.broadcast_to(jnp.sum(gate, axis=1, keepdims=True), (tile, 128))
        xr[at_, 256:span] = lower[:, 0:tail].astype(BF)

    xr[:, 0:256] = d1[0].reshape(rows, 256)
    sweep(rows, arrange)
    mine, other = c * half, (1 - c) * half

    def pre_other(at_, i):
        src = pl.ds(pl.multiple_of(other + i, tile), tile)
        sb[at_, :] = dot(xr[src, :], wgu[...]).astype(BF)

    def pre_mine(at_, i):
        src = pl.ds(pl.multiple_of(mine + i, tile), tile)
        pa[at_, :] = dot(xr[src, :], wgu[...])

    sweep(half, pre_other)
    remote(sb, rb, ss_c.at[0], rs_c.at[0], at(c_=1 - c)).start()
    sweep(half, pre_mine)
    remote(sb, rb, ss_c.at[0], rs_c.at[0], at(c_=1 - c)).wait_recv()
    for d in nby:
        p = (y + d) % ny
        part = pl.ds(pl.multiple_of(p * piece, piece), piece)
        pb[p] = (pa[part, :] + rb[part, :].astype(F32)).astype(BF)
        remote(pb.at[p], pr.at[y], ss_p.at[0, p], rs_p.at[0, y], at(y_=p)).start()

    got(lambda p: d1.at[1, p], rs_d.at[2], x, nbx, nx)
    got(lambda p: d2.at[1, p], rs_d.at[3], z, nbz, nz)
    x2[...] = d2[1].reshape(rows, 256)

    def scale(at_, _):
        lower = dot(perm[at_, :], x2[...])
        gain = prow[at_, 0:1]
        cr[at_, 256:span] = (lower[:, 0:tail] * gain).astype(BF)
        cr[at_, 0:256] = (cr[at_, 0:256].astype(F32) * gain).astype(BF)

    cr[:, 0:256] = d1[1].reshape(rows, 256)
    sweep(rows, scale)

    def dh_other(at_, i):
        src = pl.ds(pl.multiple_of(other + i, tile), tile)
        tb[at_, :] = dot_nt(cr[src, :], wdn[...]).astype(BF)

    def dh_mine(at_, i):
        src = pl.ds(pl.multiple_of(mine + i, tile), tile)
        da[at_, :] = dot_nt(cr[src, :], wdn[...])

    sweep(half, dh_other)
    remote(tb, ub, ss_c.at[1], rs_c.at[1], at(c_=1 - c)).start()
    sweep(half, dh_mine)
    remote(tb, ub, ss_c.at[1], rs_c.at[1], at(c_=1 - c)).wait_recv()
    for d in nby:
        p = (y + d) % ny
        part = pl.ds(pl.multiple_of(p * piece, piece), piece)
        vb[p] = (da[part, :] + ub[part, :].astype(F32)).astype(BF)
        remote(vb.at[p], vr.at[y], ss_p.at[1, p], rs_p.at[1, y], at(y_=p)).start()

    here = pl.ds(pl.multiple_of(y * piece, piece), piece)
    pre[...] = pa[here, :] + rb[here, :].astype(F32)
    got(lambda p: pr.at[p], rs_p.at[0], y, nby, ny)
    for d in nby:
        pre[...] += pr[(y + d) % ny].astype(F32)
    gate, up = pre[:, 0:hid], pre[:, hid : 2 * hid]
    sig = 1.0 / (1.0 + jnp.exp(-gate))
    hg[c, y] = (gate * sig * up).astype(BF)
    send_y(lambda p: hg.at[c, y], hg.at[c, y], ss_g.at[0], rs_g.at[0])
    remote(hg.at[c, y], hg.at[c, y], ss_w.at[0, y], rs_w.at[0, y], at(c_=1 - c)).start()

    dh = da[here, :] + ub[here, :].astype(F32)
    got(lambda p: vr.at[p], rs_p.at[1], y, nby, ny)
    for d in nby:
        dh += vr[(y + d) % ny].astype(F32)
    gate, up = pre[:, 0:hid], pre[:, hid : 2 * hid]
    sig = 1.0 / (1.0 + jnp.exp(-gate))
    dg[c, y, :, 0:hid] = (dh * up * sig * (1.0 + gate * (1.0 - sig))).astype(BF)
    dg[c, y, :, hid : 2 * hid] = (dh * gate * sig).astype(BF)
    send_y(lambda p: dg.at[c, y], dg.at[c, y], ss_g.at[1], rs_g.at[1])
    remote(dg.at[c, y], dg.at[c, y], ss_w.at[1, y], rs_w.at[1, y], at(c_=1 - c)).start()

    y2[:, 128:256] = jnp.zeros((rows, 128), BF)
    xt[...] = dot_nt(
        (iota((span, span), 0) == iota((span, span), 1)).astype(F32).astype(BF), xr[...]
    ).astype(BF)

    def gather(buf, i):
        for d in nby[::-1]:
            p = (y + d) % ny
            remote(buf.at[c, p], buf.at[c, p], ss_g.at[i, p], rs_g.at[i, p], at()).wait_recv()
            remote(buf.at[c, p], buf.at[c, p], ss_w.at[i, p], rs_w.at[i, p], at(c_=1 - c)).start()
        for d in [0] + nby[::-1]:
            p = (y + d) % ny
            remote(buf.at[1 - c, p], buf.at[1 - c, p], ss_w.at[i, p], rs_w.at[i, p], at()).wait_recv()

    def back(i):
        o2[i] = dot(perm[...], y2[...]).astype(BF).reshape(nz, nx * CAP, 256)
        send_z(lambda p: o2.at[i, p], e2.at[i], ss_e.at[i, 1], rs_e.at[i, 1])
        e1[i, x] = o1[i, x]
        e2[i, z] = o2[i, z]

    def merge(i):
        got(lambda p: e1.at[i, p], rs_e.at[i, 0], x, nbx, nx)
        f1[i] = dot(g1[...], e1[i].reshape(nx * nz * CAP, 256)).astype(BF).reshape(nz, rows_of, 256)
        send_z(lambda p: f1.at[i, p], k1.at[i], ss_k.at[i, 0], rs_k.at[i, 0])
        got(lambda p: e2.at[i, p], rs_e.at[i, 1], z, nbz, nz)
        f2[i] = dot(g2[...], e2[i].reshape(nx * nz * CAP, 256)).astype(BF).reshape(nx, rows_of, 256)
        send_x(lambda p: f2.at[i, p], k2.at[i], ss_k.at[i, 1], rs_k.at[i, 1])
        k1[i, z] = f1[i, z]
        k2[i, x] = f2[i, x]

    def finish(i, out):
        got(lambda p: k1.at[i, p], rs_k.at[i, 0], z, nbz, nz)
        got(lambda p: k2.at[i, p], rs_k.at[i, 1], x, nbx, nx)
        out[:, 0:256] = jnp.sum(k1[i].astype(F32), axis=0).astype(BF)
        out[:, 256:span] = jnp.sum(k2[i].astype(F32), axis=0)[:, 0:tail].astype(BF)

    gather(hg, 0)
    per = nz * CAP

    def out_y(j, _):
        at_ = pl.ds(pl.multiple_of(j * per, per), per)
        own = hg[j // (nx // 2), pl.ds(j % (nx // 2) * (ny * 2 // nx), ny * 2 // nx)].reshape(per, hid)
        value = dot(own, wdn[...]) * prow[at_, 0:1]
        o1[0, j] = value[:, 0:256].astype(BF)
        y2[at_, 0:tail] = value[:, 256:span].astype(BF)
        return 0

    lax.fori_loop(0, nx, out_y, 0)
    send_x(lambda p: o1.at[0, p], e1.at[0], ss_e.at[0, 0], rs_e.at[0, 0])
    back(0)

    gather(dg, 1)

    def out_dx(j, _):
        at_ = pl.ds(pl.multiple_of(j * per, per), per)
        own = dg[j // (nx // 2), pl.ds(j % (nx // 2) * (ny * 2 // nx), ny * 2 // nx)].reshape(per, 2 * hid)
        value = dot_nt(own, wgu[...])
        o1[1, j] = value[:, 0:256].astype(BF)
        y2[at_, 0:tail] = value[:, 256:span].astype(BF)
        return 0

    lax.fori_loop(0, nx, out_dx, 0)
    send_x(lambda p: o1.at[1, p], e1.at[1], ss_e.at[1, 0], rs_e.at[1, 0])
    back(1)
    merge(0)

    step = span // 4

    def weights(j, _):
        at_ = pl.ds(pl.multiple_of(j * step, step), step)
        grad_o[at_, :] = dot(xt[at_, :], dg[...].reshape(rows, 2 * hid)).astype(BF)
        return 0

    lax.fori_loop(0, 4, weights, 0)
    merge(1)
    finish(0, comb_o)

    sent(lambda p: s1z, ss_a.at[0], z, nbz, nz)
    sent(lambda p: s1x, ss_a.at[1], x, nbx, nx)
    sent(lambda p: cot.at[:, 0:256], ss_a.at[2], z, nbz, nz)
    sent(lambda p: c1x, ss_a.at[3], x, nbx, nx)
    for i in range(2):
        sent(lambda p: q1.at[i, p], ss_d.at[2 * i], x, nbx, nx)
        sent(lambda p: q2.at[i, p], ss_d.at[2 * i + 1], z, nbz, nz)
        sent(lambda p: o1.at[i, p], ss_e.at[i, 0], x, nbx, nx)
        sent(lambda p: o2.at[i, p], ss_e.at[i, 1], z, nbz, nz)
    for i, (flat, parts, ring) in enumerate(((sb, pb, hg), (tb, vb, dg))):
        remote(flat, flat, ss_c.at[i], ss_c.at[i], at()).wait_send()
        sent(lambda p: parts.at[p], ss_p.at[i], y, nby, ny)
        sent(lambda p: ring.at[c, y], ss_g.at[i], y, nby, ny)
        sent(lambda p: ring.at[c, p], ss_w.at[i], y, [0] + nby, ny)
    finish(1, dtok_o)
    for i in range(2):
        sent(lambda p: f1.at[i, p], ss_k.at[i, 0], z, nbz, nz)
        sent(lambda p: f2.at[i, p], ss_k.at[i, 1], x, nbx, nx)


def shards(tokens, routes, probs, cotangent, w_gate_up, w_down):
    rows_of, span = tokens.shape
    hid = w_down.shape[1]
    nx, nz, ny = NX, NZ, NY
    rows = nx * nz * CAP
    half = rows // 2
    piece = half // ny
    vm, dma = pltpu.VMEM, pltpu.SemaphoreType.DMA
    n = max(nx, nz, ny)
    scratch = [
        vm((rows_of, 384), BF), vm((rows_of, 256), BF), vm((rows_of, 256), BF),
        vm((nz, rows_of, 384), BF), vm((nx, rows_of, 256), BF),
        vm((nz, rows_of, 256), BF), vm((nx, rows_of, 256), BF),
        vm((nz * rows_of, rows), BF), vm((nx * rows_of, rows), BF),
        vm((2, nx, nz * CAP, 256), BF), vm((2, nz, nx * CAP, 256), BF),
        vm((2, nx, nz * CAP, 256), BF), vm((2, nz, nx * CAP, 256), BF),
        vm((rows, rows), BF), vm((rows, 256), BF), vm((rows, span), BF), vm((span, rows), BF),
        vm((rows, span), BF), vm((rows, 128), F32),
        vm((half, 2 * hid), F32), vm((half, 2 * hid), BF), vm((half, 2 * hid), BF),
        vm((ny, piece, 2 * hid), BF), vm((ny, piece, 2 * hid), BF),
        vm((half, hid), F32), vm((half, hid), BF), vm((half, hid), BF),
        vm((ny, piece, hid), BF), vm((ny, piece, hid), BF),
        vm((piece, 2 * hid), F32),
        vm((2, ny, piece, hid), BF), vm((2, ny, piece, 2 * hid), BF),
        vm((rows, 256), BF),
        vm((2, nx, nz * CAP, 256), BF), vm((2, nz, nx * CAP, 256), BF),
        vm((2, nx, nz * CAP, 256), BF), vm((2, nz, nx * CAP, 256), BF),
        vm((2, nz, rows_of, 256), BF), vm((2, nx, rows_of, 256), BF),
        vm((2, nz, rows_of, 256), BF), vm((2, nx, rows_of, 256), BF),
        dma((4, n)), dma((4, n)), dma((4, n)), dma((4, n)), dma((2,)), dma((2,)),
        dma((2, n)), dma((2, n)), dma((2, n)), dma((2, n)), dma((2, n)), dma((2, n)),
        dma((2, 2, n)), dma((2, 2, n)), dma((2, 2, n)), dma((2, 2, n)),
    ]
    combined, d_tokens, grad = pl.pallas_call(
        kernel,
        out_shape=(
            jax.ShapeDtypeStruct((rows_of, span), BF),
            jax.ShapeDtypeStruct((rows_of, span), BF),
            jax.ShapeDtypeStruct((span, 2 * hid), BF),
        ),
        in_specs=[pl.BlockSpec(memory_space=pltpu.VMEM)] * 6,
        out_specs=[pl.BlockSpec(memory_space=pltpu.VMEM)] * 3,
        scratch_shapes=scratch,
        compiler_params=pltpu.CompilerParams(
            collective_id=0, has_side_effects=True, vmem_limit_bytes=48 * 2**20
        ),
        name="expert_layer",
    )(tokens, cotangent, routes, probs, w_gate_up.reshape(span, 2 * hid), w_down[0])
    return combined, d_tokens, grad.reshape(1, span, 2, hid)


def solution(mesh):
    placed = (
        P("expert", "dp"),
        P("expert", None),
        P("expert", None),
        P("expert", "dp"),
        P("expert", "dp", None, None),
        P("expert", None, "dp"),
    )
    return jax.shard_map(
        shards,
        mesh=mesh,
        in_specs=placed,
        out_specs=(P("expert", "dp"), P("expert", "dp"), P("expert", "dp", None, None)),
        check_vma=False,
    )
```

time: 271 us -> 106 us (0.39); the launches traced: 266 us -> 105 us
  waiting for transfers between devices: 178 us -> 0 us
  Pallas kernels: 0 us -> 98.3 us
  starting transfers between devices: 50.6 us -> 0 us
  between operations: 14.3 us -> 0.69 us
  matrix products: 8.54 us -> 0 us
  other arithmetic: 5.02 us -> 0 us
  local copies, waits for them, and re-layouts: 9.86 us -> 6.33 us
    psum x1 -> x0, waiting for transfers between devices: 122 us -> none  [shards(): lax.psum(partial_value.astype(jnp.bfloat16), 'dp').astype(jnp.float32)]
    pallas_call x0 -> x1, Pallas kernels: none -> 98.3 us  [shards(): pl.pallas_call(kernel, out_shape=(jax.ShapeDtypeStruct((rows_of, span), B...]
    all_to_all x4 -> x0, waiting for transfers between devices: 55.3 us -> none  [the longest x1 16.7 us: shards(): lax.all_to_all(send_dy, 'expert', split_axis=0, concat_axis=0, tiled=True)]
    all_to_all x4 -> x0, starting transfers between devices: 50.6 us -> none  [the longest x1 23.2 us: shards(): lax.all_to_all(send_dy, 'expert', split_axis=0, concat_axis=0, tiled=True)]
    dot_general x11 -> x0, matrix products: 8.54 us -> none  [the longest x1 1.86 us: shards(): jnp.einsum('rd,rgh->dgh', rows_x, d_pre, preferred_element_type=jnp.float32)]
    convert_element_type x4 -> x0, local copies, waits for them, and re-layouts: 3.3 us -> none  [the longest x1 2.02 us: shards(): jnp.dot(hidden, w_dn, preferred_element_type=jnp.float32)]
  transfers between devices with their start and end apart: 5 -> 0, of which waited for: 5 -> 0; matrix products, arithmetic and copies ran while one was open for 3% -> 0% of each run, Pallas kernels for 0% -> 0%
where the time goes in v1:
time: 106 us; the launch traced here: 105 us
  Pallas kernels  98.3 us (93%)
  local copies, waits for them, and re-layouts  6.33 us (6%)
    pallas_call x1, Pallas kernels, shards(): pl.pallas_call(kernel, out_shape=(jax.ShapeDtypeStruct((rows_of, span), B...  98.3 us
    unnamed x12, local copies, waits for them, and re-layouts  4.74 us

profile of v1, /device:TPU:1, one launch (start us, length us, event | category | flops | bytes accessed | tf_op | source)
XLA Modules:
  0.0 105.3 jit_solution(11146738296855125932)
XLA Ops:
  0.6 0.0 copy-start.2
  0.6 0.8 copy.10.routes
  1.5 0.8 copy.11.probs
  2.2 1.2 %copy.9 = bf16[1,512,448]{2,1,0:T(8,128)(2,1)S(1)} copy(bf16[1,512,448]{1,2,0:T(8,128)(2,1)} %param.11) | data formatting | bytes 917504 | tf_op args[5]
  3.5 0.0 copy-done.2
  3.5 0.0 copy-start
  3.5 0.0 copy-start.1
  3.5 0.2 copy.12
  3.7 0.5 copy-done
  4.2 0.0 copy-done.1
  4.2 98.3 %expert_layer.1 = (bf16[16,448]{1,0:T(8,128)(2,1)S(1)}, bf16[16,448]{1,0:T(8,128)(2,1)S(1)}, bf16[448,1024]{1,0:T(8,128)(2,1)S(1)}) custom-call(bf16[16,448]{1,0:T(8,128)(2,1)S(1)} %copy-done, bf16[16,448]{1,0:T(8,128)(2,1)S(1)} %copy-done.1, s32[16,8]{1,0:T(8,128)S(1)} %copy.10.routes, f32[16,8]{1,0:T(8,128)S(1)} %copy.11.probs, ...), custom_call_target="tpu_custom_call" | custom-call | tf_op jit(solution)/shard_map/expert_layer/pallas_call | solution.py:398
  102.5 1.6 %reshape.13 = bf16[1,448,2,512]{3,2,1,0:T(2,128)(2,1)} reshape(bf16[448,1024]{1,0:T(8,128)(2,1)S(1)} %get-tuple-element.8) | data formatting | bytes 1835008 | tf_op jit(solution)/shard_map/reshape | solution.py:413
  104.1 0.6 copy.15
  104.7 0.6 copy.16
Async XLA Ops:
  0.6 2.8 %copy-start.2 = (bf16[1,448,2,512]{3,2,1,0:T(2,128)(2,1)S(1)}, bf16[1,448,2,512]{3,2,1,0:T(2,128)(2,1)}, u32[]{:S(2)}) copy-start(bf16[1,448,2,512]{3,2,1,0:T(2,128)(2,1)} %param.10) | copy-start | bytes 2752516
  3.5 0.7 copy-start
  3.5 0.7 copy-start.1

commit v2 on v1

v2 whole, which is shorter than its diff:
```python
import functools

import jax
import jax.numpy as jnp
from jax import lax
from jax.experimental import pallas as pl
from jax.experimental.pallas import tpu as pltpu
from jax.sharding import PartitionSpec as P

CAP = 8
PARTS = 2
SUB = CAP // PARTS
NX = 8
NZ = 8
NY = 8
BF = jnp.bfloat16
F32 = jnp.float32
MESH = pl.DeviceIdType.MESH
ORDER = (4, 3, 5, 2, 6, 1, 7)


def iota(shape, dim):
    return lax.broadcasted_iota(jnp.int32, shape, dim)


def dot(a, b):
    return jnp.dot(a, b, preferred_element_type=F32)


def dot_nt(a, b):
    return lax.dot_general(a, b, (((1,), (1,)), ((), ())), preferred_element_type=F32)


def dot_tn(a, b):
    return lax.dot_general(a, b, (((0,), (0,)), ((), ())), preferred_element_type=F32)


def rank_table(meta, rows_of):
    n = meta.shape[0]
    mask = (meta > 0).astype(F32)
    i, j = iota((n, n), 0), iota((n, n), 1)
    lower = ((i // rows_of == j // rows_of) & (j < i)).astype(F32).astype(BF)
    rank = dot(lower, mask.astype(BF))
    return jnp.where(mask > 0, rank, -1.0).astype(BF)


def place_table(table, expert_of, blocks, rows_of):
    n = table.shape[0]
    width = expert_of.shape[1]
    select = (iota((128, width), 0) == 64 + expert_of).astype(F32).astype(BF)
    rank = dot(table, select)
    col = iota((n, width), 1)
    row = iota((n, width), 0) // rows_of
    slot = col // (width // PARTS) * SUB + col % SUB
    return ((rank == slot.astype(F32)) & (col // SUB % blocks == row)).astype(F32).astype(BF)


def kernel(
    tok, cot, routes, probs, wgu, wdn, comb_o, dtok_o, grad_o,
    s1z, s1x, c1x, a1z, a1x, b1z, b1x, g1, g2, q1, q2, d1, d2, perm, x2, xr, xt, cr, prow,
    pa, sb, rb, pb, pq, pr, da, tb, ub, vb, vq, vr, pre, hg, dg, y2, o1, o2, e1, e2, f1, f2, k1, k2,
    ss_a, rs_a, ss_d, rs_d, ss_c, rs_c, ss_q, rs_q, ss_p, rs_p, ss_g, rs_g, ss_w, rs_w, ss_e, rs_e, ss_k, rs_k,
):
    nx, nz, ny = NX, NZ, NY
    dp, ex = lax.axis_index("dp"), lax.axis_index("expert")
    y, c = dp // 2, dp % 2
    z, x = ex // nx, ex % nx
    rows_of, span = tok.shape
    tail = span - 256
    rows = nz * nx * SUB
    half = rows // 2
    piece = half // ny
    hid = wdn.shape[1]
    tile = min(128, half)
    nbx, nbz = [d for d in ORDER if d < nx], [d for d in ORDER if d < nz]

    def at(y_=None, c_=None, z_=None, x_=None):
        return (
            (y if y_ is None else y_) * 2 + (c if c_ is None else c_),
            (z if z_ is None else z_) * nx + (x if x_ is None else x_),
        )

    def remote(src, dst, ss, rs, dev):
        return pltpu.make_async_remote_copy(
            src_ref=src, dst_ref=dst, send_sem=ss, recv_sem=rs, device_id=dev, device_id_type=MESH
        )

    def send_x(src, dst, ss, rs):
        for d in nbx:
            p = (x + d) % nx
            remote(src(p), dst.at[x], ss.at[p], rs.at[x], at(x_=p)).start()

    def send_z(src, dst, ss, rs):
        for d in nbz:
            p = (z + d) % nz
            remote(src(p), dst.at[z], ss.at[p], rs.at[z], at(z_=p)).start()

    def lanes(ref, cut):
        w = ref.shape[-1]
        return (pl.ds(0, w), pl.ds(0, w // 2), pl.ds(w // 2, w // 2))[cut]

    relays = ((2, 4, 1), (-2, -4, 2), (1, 3, 0), (-1, -3, 0))

    def near(d):
        return (y + d) % ny

    def reduce_first(i, value, out, land):
        for j, (d, far, cut) in enumerate(relays):
            out[j] = value(near(far)).astype(BF)
            at_ = lanes(out, cut)
            remote(out.at[j, :, at_], land.at[j, :, at_], ss_q.at[i, j], rs_q.at[i, j], at(y_=near(d))).start()

    def reduce_next(i, value, out, final):
        for j, d in ((0, 1), (1, -1)):
            out[4 + j] = value(near(d)).astype(BF)
            remote(out.at[4 + j], final.at[j], ss_p.at[i, j], rs_p.at[i, j], at(y_=near(d))).start()

    def reduce_relay(i, value, out, land, final):
        for j, d in ((2, 2), (3, -2)):
            part, whole = j - 2, j
            cut = lanes(land, j - 1)
            for ref, k in ((land.at[part, :, cut], part), (land.at[whole], whole)):
                remote(ref, ref, rs_q.at[i, k], rs_q.at[i, k], at()).wait_recv()
            total = value(near(d)) + land[whole].astype(F32)
            w = total.shape[1] // 2
            left, right = total[:, :w], total[:, w:]
            more = land[part, :, cut].astype(F32)
            out[4 + j, :, 0:w] = (left + more if j == 2 else left).astype(BF)
            out[4 + j, :, w : 2 * w] = (right if j == 2 else right + more).astype(BF)
            remote(out.at[4 + j], final.at[j], ss_p.at[i, j], rs_p.at[i, j], at(y_=near(d))).start()

    def reduce_done(i, total, final):
        for j in range(4):
            remote(final.at[j], final.at[j], rs_p.at[i, j], rs_p.at[i, j], at()).wait_recv()
            total += final[j].astype(F32)
        return total

    def reduce_sent(i, out):
        for j, (_, _, cut) in enumerate(relays):
            ref = out.at[j, :, lanes(out, cut)]
            remote(ref, ref, ss_q.at[i, j], ss_q.at[i, j], at()).wait_send()
            remote(out.at[4 + j], out.at[4 + j], ss_p.at[i, j], ss_p.at[i, j], at()).wait_send()

    hops = ((0, 2, 0), (0, -2, 0), (0, 1, 0), (0, -1, 0), (-2, 2, 1), (2, -2, 2), (-2, 1, 0), (2, -1, 0))
    origins = ((-2, 0), (2, 0), (-1, 0), (1, 0), (-4, 1), (4, 2), (-3, 0), (3, 0))

    def gather_send(i, buf, which):
        for k in which:
            origin, d, cut = hops[k]
            ref = buf.at[c, near(origin), :, lanes(buf, cut)]
            remote(ref, ref, ss_g.at[i, k], rs_g.at[i, k], at(y_=near(d))).start()

    def gather_got(i, buf, k):
        origin, cut = origins[k]
        ref = buf.at[c, near(origin), :, lanes(buf, cut)]
        remote(ref, ref, rs_g.at[i, k], rs_g.at[i, k], at()).wait_recv()

    def pass_on(i, buf, d):
        ref = buf.at[c, near(d)]
        remote(ref, ref, ss_w.at[i, near(d)], rs_w.at[i, near(d)], at(c_=1 - c)).start()

    def gather_first(i, buf):
        gather_send(i, buf, (0, 1, 2, 3))
        pass_on(i, buf, 0)

    def gather_relay(i, buf):
        gather_got(i, buf, 0)
        gather_send(i, buf, (4, 6))
        gather_got(i, buf, 1)
        gather_send(i, buf, (5, 7))
        pass_on(i, buf, -2)
        pass_on(i, buf, 2)
        for k, d in ((2, -1), (3, 1)):
            gather_got(i, buf, k)
            pass_on(i, buf, d)

    def gather_done(i, buf):
        for k, d in ((6, -3), (7, 3)):
            gather_got(i, buf, k)
            pass_on(i, buf, d)
        gather_got(i, buf, 4)
        gather_got(i, buf, 5)
        pass_on(i, buf, 4)
        for d in (0, -2, 2, -1, 1, -3, 3, 4):
            ref = buf.at[1 - c, near(d)]
            remote(ref, ref, rs_w.at[i, near(d)], rs_w.at[i, near(d)], at()).wait_recv()

    def gather_sent(i, buf):
        for k, (origin, _, cut) in enumerate(hops):
            ref = buf.at[c, near(origin), :, lanes(buf, cut)]
            remote(ref, ref, ss_g.at[i, k], ss_g.at[i, k], at()).wait_send()
        for d in range(ny):
            ref = buf.at[c, near(d)]
            remote(ref, ref, ss_w.at[i, near(d)], ss_w.at[i, near(d)], at()).wait_send()

    def got(dst, rs, me, others, n):
        for d in others[::-1]:
            p = (me + d) % n
            remote(dst(p), dst(p), rs.at[p], rs.at[p], at()).wait_recv()

    def sent(src, ss, me, others, n):
        for d in others:
            p = (me + d) % n
            remote(src(p), src(p), ss.at[p], ss.at[p], at()).wait_send()

    barrier = pltpu.get_barrier_semaphore()
    for d in nbx:
        pl.semaphore_signal(barrier, 1, device_id=at(x_=(x + d) % nx), device_id_type=MESH)
    for d in nbz:
        pl.semaphore_signal(barrier, 1, device_id=at(z_=(z + d) % nz), device_id_type=MESH)
    for d in (1, -1, 2, -2):
        pl.semaphore_signal(barrier, 1, device_id=at(y_=(y + d) % ny), device_id_type=MESH)
    pl.semaphore_signal(barrier, 1, device_id=at(c_=1 - c), device_id_type=MESH)

    weight = jnp.zeros((32, rows_of), F32)
    for k in range(routes.shape[0]):
        weight += jnp.where(routes[k : k + 1, :] == iota((32, rows_of), 0), probs[k : k + 1, :], 0.0)
    high = weight.astype(BF)
    low = (weight - high.astype(F32)).astype(BF)
    lane = iota((32, 128), 1) - iota((32, 128), 0)
    meta = dot_tn(high, (lane == 64).astype(F32).astype(BF)) + dot_tn(low, (lane == 96).astype(F32).astype(BF))
    s1z[:, 0:256] = tok[:, 0:256]
    s1z[:, 256:384] = meta.astype(BF)
    s1x[...] = jnp.zeros_like(s1x)
    s1x[:, 0:tail] = tok[:, 256:span]
    s1x[:, 128:256] = (s1x[:, 128:256].astype(F32) + meta).astype(BF)
    c1x[...] = jnp.zeros_like(c1x)
    c1x[:, 0:tail] = cot[:, 256:span]
    pl.semaphore_wait(barrier, len(nbx) + len(nbz) + 5)

    send_z(lambda p: s1z, a1z, ss_a.at[0], rs_a.at[0])
    send_x(lambda p: s1x, a1x, ss_a.at[1], rs_a.at[1])
    send_z(lambda p: cot.at[:, 0:256], b1z, ss_a.at[2], rs_a.at[2])
    send_x(lambda p: c1x, b1x, ss_a.at[3], rs_a.at[3])
    a1z[z] = s1z[...]
    a1x[x] = s1x[...]
    b1z[z] = cot[:, 0:256]
    b1x[x] = c1x[...]
    r_, c_ = iota((rows, rows), 0), iota((rows, rows), 1)
    perm[...] = (
        (r_ // SUB // nz == c_ // SUB % nx) & (r_ // SUB % nz == c_ // SUB // nx) & (r_ % SUB == c_ % SUB)
    ).astype(F32).astype(BF)

    wide = (1, PARTS * rows)
    dest = iota(wide, 1) % rows

    def pack(g, block, q):
        q[...] = dot_tn(g[...], block).astype(BF).reshape(q.shape)

    def slots_x(i, h):
        send_x(lambda p: q1.at[i, h, p], d1.at[i, h], ss_d.at[0, i, h], rs_d.at[0, i, h])
        d1[i, h, x] = q1[i, h, x]

    def slots_z(i, h):
        send_z(lambda p: q2.at[i, h, p], d2.at[i, h], ss_d.at[1, i, h], rs_d.at[1, i, h])
        d2[i, h, z] = q2[i, h, z]

    got(lambda p: a1z.at[p], rs_a.at[0], z, nbz, nz)
    block = a1z[...].reshape(nz * rows_of, 384)
    table = rank_table(block[:, 256:384].astype(F32), rows_of)
    g1[...] = place_table(table, z * (nx // 2) + dest // (nz * SUB) // 2, nz, rows_of)
    pack(g1, block[:, 0:256], q1.at[0])
    slots_x(0, 0)
    got(lambda p: a1x.at[p], rs_a.at[1], x, nbx, nx)
    block = a1x[...].reshape(nx * rows_of, 256)
    table = rank_table(block[:, 128:256].astype(F32) * (iota((nx * rows_of, 128), 1) >= 64), rows_of)
    g2[...] = place_table(table, dest // (nx * SUB) * (nx // 2) + x // 2, nx, rows_of)
    pack(g2, block, q2.at[0])
    slots_z(0, 0)
    slots_x(0, 1)
    slots_z(0, 1)
    got(lambda p: b1z.at[p], rs_a.at[2], z, nbz, nz)
    pack(g1, b1z[...].reshape(nz * rows_of, 256), q1.at[1])
    got(lambda p: b1x.at[p], rs_a.at[3], x, nbx, nx)
    pack(g2, b1x[...].reshape(nx * rows_of, 256), q2.at[1])
    for h in range(PARTS):
        slots_x(1, h)
        slots_z(1, h)

    def sweep(n, body):
        def step(i, _):
            body(pl.ds(pl.multiple_of(i * tile, tile), tile), i * tile)
            return 0

        lax.fori_loop(0, n // tile, step, 0)

    expert = z * (nx // 2) + x // 2
    mine, other = c * half, (1 - c) * half
    y2[:, :, 128:256] = jnp.zeros((PARTS, rows, 128), BF)

    def slots_got(i, h):
        got(lambda p: d1.at[i, h, p], rs_d.at[0, i, h], x, nbx, nx)
        got(lambda p: d2.at[i, h, p], rs_d.at[1, i, h], z, nbz, nz)

    def parts_of(src, weights, near_, far_, back_, i):
        def far_rows(at_, k):
            far_[at_, :] = dot(src[pl.ds(pl.multiple_of(other + k, tile), tile), :], weights[...]).astype(BF)

        def near_rows(at_, k):
            near_[at_, :] = dot(src[pl.ds(pl.multiple_of(mine + k, tile), tile), :], weights[...])

        sweep(half, far_rows)
        remote(far_, back_, ss_c.at[i], rs_c.at[i], at(c_=1 - c)).start()
        sweep(half, near_rows)

    def tokens_in(h):
        slots_got(0, h)
        x2[...] = d2[0, h].reshape(rows, 256)
        xr[h, :, 0:256] = d1[0, h].reshape(rows, 256)

        def arrange(at_, _):
            lower = dot(perm[at_, :], x2[...])
            gate = lower[:, 128:256]
            which = iota((tile, 128), 1)
            gate = jnp.where((which == 64 + expert) | (which == 96 + expert), gate, 0.0)
            prow[h, at_, :] = jnp.broadcast_to(jnp.sum(gate, axis=1, keepdims=True), (tile, 128))
            xr[h, at_, 256:span] = lower[:, 0:tail].astype(BF)

        sweep(rows, arrange)
        parts_of(xr.at[h], wgu, pa.at[h], sb.at[h], rb.at[h], h)

    def grads_in(h):
        slots_got(1, h)
        x2[...] = d2[1, h].reshape(rows, 256)
        cr[:, 0:256] = d1[1, h].reshape(rows, 256)

        def scale(at_, _):
            lower = dot(perm[at_, :], x2[...])
            gain = prow[h, at_, 0:1]
            cr[at_, 256:span] = (lower[:, 0:tail] * gain).astype(BF)
            cr[at_, 0:256] = (cr[at_, 0:256].astype(F32) * gain).astype(BF)

        sweep(rows, scale)
        parts_of(cr, wdn, da.at[h], tb.at[h], ub.at[h], 2 + h)

    def pre_sum(h):
        def value(p):
            part = pl.ds(pl.multiple_of(p * piece, piece), piece)
            return pa[h, part, :] + rb[h, part, :].astype(F32)

        return value

    def dh_sum(h):
        def value(p):
            part = pl.ds(pl.multiple_of(p * piece, piece), piece)
            return da[h, part, :] + ub[h, part, :].astype(F32)

        return value

    def pre_first(h):
        remote(rb.at[h], rb.at[h], rs_c.at[h], rs_c.at[h], at()).wait_recv()
        reduce_first(h, pre_sum(h), pb.at[h], pq.at[h])
        reduce_next(h, pre_sum(h), pb.at[h], pr.at[h])

    def dh_first(h):
        remote(ub.at[h], ub.at[h], rs_c.at[2 + h], rs_c.at[2 + h], at()).wait_recv()
        reduce_first(2 + h, dh_sum(h), vb.at[h], vq.at[h])
        reduce_next(2 + h, dh_sum(h), vb.at[h], vr.at[h])

    def pre_relay(h):
        reduce_relay(h, pre_sum(h), pb.at[h], pq.at[h], pr.at[h])

    def dh_relay(h):
        reduce_relay(2 + h, dh_sum(h), vb.at[h], vq.at[h], vr.at[h])

    def pre_done(h):
        pre[h] = reduce_done(h, pre_sum(h)(y), pr.at[h])
        gate, up = pre[h, :, 0:hid], pre[h, :, hid : 2 * hid]
        sig = 1.0 / (1.0 + jnp.exp(-gate))
        hg[h, c, y] = (gate * sig * up).astype(BF)
        gather_first(h, hg.at[h])

    def dh_done(h):
        dh = reduce_done(2 + h, dh_sum(h)(y), vr.at[h])
        gate, up = pre[h, :, 0:hid], pre[h, :, hid : 2 * hid]
        sig = 1.0 / (1.0 + jnp.exp(-gate))
        dg[h, c, y, :, 0:hid] = (dh * up * sig * (1.0 + gate * (1.0 - sig))).astype(BF)
        dg[h, c, y, :, hid : 2 * hid] = (dh * gate * sig).astype(BF)
        gather_first(2 + h, dg.at[h])

    def back(i, h, product, buf):
        full = buf[h].reshape(rows, buf.shape[-1])
        ways = tile // (nz * SUB)
        for j in range(rows // tile):
            value = product(full[j * tile : (j + 1) * tile], pl.ds(j * tile, tile))
            o1[i, h, j * ways : (j + 1) * ways] = value[:, 0:256].astype(BF).reshape(ways, nz * SUB, 256)
            y2[h, j * tile : (j + 1) * tile, 0:tail] = value[:, 256:span].astype(BF)
        send_x(lambda p: o1.at[i, h, p], e1.at[i, h], ss_e.at[0, i, h], rs_e.at[0, i, h])
        o2[i, h] = dot(perm[...], y2[h]).astype(BF).reshape(nz, nx * SUB, 256)
        send_z(lambda p: o2.at[i, h, p], e2.at[i, h], ss_e.at[1, i, h], rs_e.at[1, i, h])
        e1[i, h, x] = o1[i, h, x]
        e2[i, h, z] = o2[i, h, z]

    def back_y(h):
        back(0, h, lambda own, at_: dot_nt(own, wdn[...]) * prow[h, at_, 0:1], hg)

    def back_dx(h):
        back(1, h, lambda own, at_: dot_nt(own, wgu[...]), dg)

    def merge(i):
        for h in range(PARTS):
            got(lambda p: e1.at[i, h, p], rs_e.at[0, i, h], x, nbx, nx)
        f1[i] = dot(g1[...], e1[i].reshape(PARTS * rows, 256)).astype(BF).reshape(nz, rows_of, 256)
        send_z(lambda p: f1.at[i, p], k1.at[i], ss_k.at[i, 0], rs_k.at[i, 0])
        for h in range(PARTS):
            got(lambda p: e2.at[i, h, p], rs_e.at[1, i, h], z, nbz, nz)
        f2[i] = dot(g2[...], e2[i].reshape(PARTS * rows, 256)).astype(BF).reshape(nx, rows_of, 256)
        send_x(lambda p: f2.at[i, p], k2.at[i], ss_k.at[i, 1], rs_k.at[i, 1])
        k1[i, z] = f1[i, z]
        k2[i, x] = f2[i, x]

    def finish(i, out):
        got(lambda p: k1.at[i, p], rs_k.at[i, 0], z, nbz, nz)
        got(lambda p: k2.at[i, p], rs_k.at[i, 1], x, nbx, nx)
        out[:, 0:256] = jnp.sum(k1[i].astype(F32), axis=0).astype(BF)
        out[:, 256:span] = jnp.sum(k2[i].astype(F32), axis=0)[:, 0:tail].astype(BF)

    tokens_in(0)
    tokens_in(1)
    pre_first(0)
    grads_in(0)
    pre_first(1)
    dh_first(0)
    grads_in(1)
    pre_relay(0)
    dh_first(1)
    pre_relay(1)
    dh_relay(0)
    pre_done(0)
    dh_relay(1)
    pre_done(1)
    dh_done(0)
    gather_relay(0, hg.at[0])
    dh_done(1)
    gather_relay(1, hg.at[1])
    gather_relay(2, dg.at[0])
    gather_done(0, hg.at[0])
    back_y(0)
    gather_relay(3, dg.at[1])
    gather_done(1, hg.at[1])
    back_y(1)
    gather_done(2, dg.at[0])
    back_dx(0)
    gather_done(3, dg.at[1])
    back_dx(1)

    eye = (iota((span, span), 0) == iota((span, span), 1)).astype(F32).astype(BF)
    xt[...] = dot_nt(eye, xr[...].reshape(PARTS * rows, span)).astype(BF)
    step = span // 4

    def weights(j, _):
        at_ = pl.ds(pl.multiple_of(j * step, step), step)
        value = dot(xt[at_, :], dg[...].reshape(PARTS * rows, 2 * hid))
        for k in range(2):
            part = value[:, k * hid : (k + 1) * hid]
            grad_o[pl.ds(j * (step // 8), step // 8), k] = part.reshape(step // 8, 8, hid).astype(BF)
        return 0

    lax.fori_loop(0, 4, weights, 0)
    merge(0)
    merge(1)
    finish(0, comb_o)

    sent(lambda p: s1z, ss_a.at[0], z, nbz, nz)
    sent(lambda p: s1x, ss_a.at[1], x, nbx, nx)
    sent(lambda p: cot.at[:, 0:256], ss_a.at[2], z, nbz, nz)
    sent(lambda p: c1x, ss_a.at[3], x, nbx, nx)
    for h in range(PARTS):
        for i in range(2):
            sent(lambda p: q1.at[i, h, p], ss_d.at[0, i, h], x, nbx, nx)
            sent(lambda p: q2.at[i, h, p], ss_d.at[1, i, h], z, nbz, nz)
            sent(lambda p: o1.at[i, h, p], ss_e.at[0, i, h], x, nbx, nx)
            sent(lambda p: o2.at[i, h, p], ss_e.at[1, i, h], z, nbz, nz)
        for i, (flat, parts, ring) in enumerate(((sb, pb, hg), (tb, vb, dg))):
            j = 2 * i + h
            remote(flat.at[h], flat.at[h], ss_c.at[j], ss_c.at[j], at()).wait_send()
            reduce_sent(j, parts.at[h])
            gather_sent(j, ring.at[h])
    finish(1, dtok_o)
    for i in range(2):
        sent(lambda p: f1.at[i, p], ss_k.at[i, 0], z, nbz, nz)
        sent(lambda p: f2.at[i, p], ss_k.at[i, 1], x, nbx, nx)


def shards(tokens, routes, probs, cotangent, w_gate_up, w_down):
    rows_of, span = tokens.shape
    hid = w_down.shape[1]
    nx, nz, ny = NX, NZ, NY
    rows = nx * nz * SUB
    half = rows // 2
    piece = half // ny
    vm, dma = pltpu.VMEM, pltpu.SemaphoreType.DMA
    n = max(nx, nz, ny)
    h = PARTS
    along_x, along_z = vm((2, h, nx, nz * SUB, 256), BF), vm((2, h, nz, nx * SUB, 256), BF)
    scratch = [
        vm((rows_of, 384), BF), vm((rows_of, 256), BF), vm((rows_of, 256), BF),
        vm((nz, rows_of, 384), BF), vm((nx, rows_of, 256), BF),
        vm((nz, rows_of, 256), BF), vm((nx, rows_of, 256), BF),
        vm((nz * rows_of, h * rows), BF), vm((nx * rows_of, h * rows), BF),
        along_x, along_z, along_x, along_z,
        vm((rows, rows), BF), vm((rows, 256), BF), vm((h, rows, span), BF), vm((span, h * rows), BF),
        vm((rows, span), BF), vm((h, rows, 128), F32),
        vm((h, half, 2 * hid), F32), vm((h, half, 2 * hid), BF), vm((h, half, 2 * hid), BF),
        vm((h, 8, piece, 2 * hid), BF), vm((h, 4, piece, 2 * hid), BF), vm((h, 4, piece, 2 * hid), BF),
        vm((h, half, hid), F32), vm((h, half, hid), BF), vm((h, half, hid), BF),
        vm((h, 8, piece, hid), BF), vm((h, 4, piece, hid), BF), vm((h, 4, piece, hid), BF),
        vm((h, piece, 2 * hid), F32),
        vm((h, 2, ny, piece, hid), BF), vm((h, 2, ny, piece, 2 * hid), BF),
        vm((h, rows, 256), BF),
        along_x, along_z, along_x, along_z,
        vm((2, nz, rows_of, 256), BF), vm((2, nx, rows_of, 256), BF),
        vm((2, nz, rows_of, 256), BF), vm((2, nx, rows_of, 256), BF),
        dma((4, n)), dma((4, n)), dma((2, 2, h, n)), dma((2, 2, h, n)), dma((2 * h,)), dma((2 * h,)),
        dma((2 * h, 4)), dma((2 * h, 4)), dma((2 * h, 4)), dma((2 * h, 4)),
        dma((2 * h, 8)), dma((2 * h, 8)), dma((2 * h, n)), dma((2 * h, n)),
        dma((2, 2, h, n)), dma((2, 2, h, n)), dma((2, 2, n)), dma((2, 2, n)),
    ]
    combined, d_tokens, grad = pl.pallas_call(
        kernel,
        out_shape=(
            jax.ShapeDtypeStruct((rows_of, span), BF),
            jax.ShapeDtypeStruct((rows_of, span), BF),
            jax.ShapeDtypeStruct((span // 8, 2, 8, hid), BF),
        ),
        in_specs=[pl.BlockSpec(memory_space=pltpu.VMEM)] * 6,
        out_specs=[pl.BlockSpec(memory_space=pltpu.VMEM)] * 3,
        scratch_shapes=scratch,
        compiler_params=pltpu.CompilerParams(
            collective_id=0, has_side_effects=True, vmem_limit_bytes=48 * 2**20
        ),
        name="expert_layer",
    )(tokens, cotangent, routes.T, probs.T, w_gate_up.reshape(span, 2 * hid), w_down[0].T)
    return combined, d_tokens, grad.transpose(0, 2, 1, 3).reshape(1, span, 2, hid)


def solution(mesh):
    placed = (
        P("expert", "dp"),
        P("expert", None),
        P("expert", None),
        P("expert", "dp"),
        P("expert", "dp", None, None),
        P("expert", None, "dp"),
    )
    return jax.shard_map(
        shards,
        mesh=mesh,
        in_specs=placed,
        out_specs=(P("expert", "dp"), P("expert", "dp"), P("expert", "dp", None, None)),
        check_vma=False,
    )
```

time: 106 us -> 89.8 us (0.85)
  Pallas kernels: 98.3 us -> 84.3 us
  local copies, waits for them, and re-layouts: 6.33 us -> 4.58 us
    pallas_call x1, Pallas kernels: 98.3 us -> 84.3 us  [shards(): pl.pallas_call(kernel, out_shape=(jax.ShapeDtypeStruct((rows_of, span), B...]
    reshape x1, local copies, waits for them, and re-layouts: 1.59 us -> 0.06 us  [shards(): grad.transpose(0, 2, 1, 3).reshape(1, span, 2, hid)]
    unnamed x12 -> x14, local copies, waits for them, and re-layouts: 4.74 us -> 4.51 us
where the time goes in v2:
time: 89.8 us; the launch traced here: 89.6 us
  Pallas kernels  84.3 us (94%)
  local copies, waits for them, and re-layouts  4.58 us (5%)
    pallas_call x1, Pallas kernels, shards(): pl.pallas_call(kernel, out_shape=(jax.ShapeDtypeStruct((rows_of, span), B...  84.3 us
    unnamed x14, local copies, waits for them, and re-layouts  4.51 us

profile of v2, /device:TPU:1, one launch (start us, length us, event | category | flops | bytes accessed | tf_op | source)
XLA Modules:
  0.0 89.6 jit_solution(5166771972721241249)
XLA Ops:
  0.6 0.0 copy-start
  0.6 0.0 copy-start.1
  0.7 0.0 copy-start.2
  0.7 0.0 copy-start.3
  0.7 0.0 copy-start.4
  0.7 1.4 %copy.11 = bf16[56,8,2,512]{3,1,2,0:T(8,128)(2,1)S(1)} copy(bf16[56,8,2,512]{3,2,1,0:T(2,128)(2,1)} %bitcast.17) | data formatting | bytes 1835008
  2.1 0.0 copy-done
  2.1 0.0 copy-done.1
  2.1 0.0 copy-done.2
  2.1 0.0 copy-done.3
  2.1 0.0 copy-done.4
  2.2 84.3 %expert_layer.1 = (bf16[16,448]{1,0:T(8,128)(2,1)S(1)}, bf16[16,448]{1,0:T(8,128)(2,1)S(1)}, bf16[56,2,8,512]{3,2,1,0:T(8,128)(2,1)S(1)}) custom-call(bf16[16,448]{1,0:T(8,128)(2,1)S(1)} %copy-done.1, bf16[16,448]{1,0:T(8,128)(2,1)S(1)} %copy-done.2, s32[8,16]{1,0:T(8,128)S(1)} %bitcast.15, f32[8,16]{1,0:T(8,128)S(1)} %bitcast.16, ...), custom_call_target="tpu_custom_call" | custom-call | tf_op jit(solution)/shard_map/expert_layer/pallas_call | solution.py:519
  86.5 0.1 copy_bitcast_fusion
  86.5 1.9 %copy.10 = bf16[1,448,2,512]{3,2,1,0:T(2,128)(2,1)} copy(bf16[1,448,2,512]{3,1,2,0:T(8,128)(2,1)S(1)} %copy_bitcast_fusion) | data formatting | bytes 1835008
  88.4 0.6 copy.15
  89.0 0.6 copy.16
Async XLA Ops:
  0.6 1.5 %copy-start = (bf16[1,512,448]{1,2,0:T(8,128)(2,1)S(1)}, bf16[1,512,448]{1,2,0:T(8,128)(2,1)}, u32[]{:S(2)}) copy-start(bf16[1,512,448]{1,2,0:T(8,128)(2,1)} %param.11) | copy-start | bytes 1376260
  0.6 1.5 %copy-start.1 = (bf16[16,448]{1,0:T(8,128)(2,1)S(1)}, bf16[16,448]{1,0:T(8,128)(2,1)}, u32[]{:S(2)}) copy-start(bf16[16,448]{1,0:T(8,128)(2,1)} %tok.1) | copy-start | bytes 43012
  0.7 1.5 %copy-start.2 = (bf16[16,448]{1,0:T(8,128)(2,1)S(1)}, bf16[16,448]{1,0:T(8,128)(2,1)}, u32[]{:S(2)}) copy-start(bf16[16,448]{1,0:T(8,128)(2,1)} %cot.1) | copy-start | bytes 43012
  0.7 1.5 %copy-start.3 = (s32[16,8]{0,1:T(8,128)S(1)}, s32[16,8]{0,1:T(8,128)}, u32[]{:S(2)}) copy-start(s32[16,8]{0,1:T(8,128)} %param.7) | copy-start | bytes 1540
  0.7 1.5 %copy-start.4 = (f32[16,8]{0,1:T(8,128)S(1)}, f32[16,8]{0,1:T(8,128)}, u32[]{:S(2)}) copy-start(f32[16,8]{0,1:T(8,128)} %param.8) | copy-start | bytes 1540

commit v3 on v2

--- a/solution.py
+++ b/solution.py
@@ -17,6 +17,8 @@
 F32 = jnp.float32
 MESH = pl.DeviceIdType.MESH
 ORDER = (4, 3, 5, 2, 6, 1, 7)
+DIRECT = ()
+SPREAD = ()
 
 
 def iota(shape, dim):
@@ -35,29 +37,22 @@
     return lax.dot_general(a, b, (((0,), (0,)), ((), ())), preferred_element_type=F32)
 
 
-def rank_table(meta, rows_of):
-    n = meta.shape[0]
+def rank_table(meta, lower):
     mask = (meta > 0).astype(F32)
-    i, j = iota((n, n), 0), iota((n, n), 1)
-    lower = ((i // rows_of == j // rows_of) & (j < i)).astype(F32).astype(BF)
-    rank = dot(lower, mask.astype(BF))
-    return jnp.where(mask > 0, rank, -1.0).astype(BF)
-
-
-def place_table(table, expert_of, blocks, rows_of):
-    n = table.shape[0]
-    width = expert_of.shape[1]
-    select = (iota((128, width), 0) == 64 + expert_of).astype(F32).astype(BF)
-    rank = dot(table, select)
-    col = iota((n, width), 1)
-    row = iota((n, width), 0) // rows_of
-    slot = col // (width // PARTS) * SUB + col % SUB
-    return ((rank == slot.astype(F32)) & (col // SUB % blocks == row)).astype(F32).astype(BF)
+    return jnp.where(mask > 0, dot(lower, mask.astype(BF)), -1.0).astype(BF)
+
+
+def place_plan(expert_of, blocks, rows_of, select, want):
+    n, width = want.shape
+    select[...] = (iota((128, width), 0) == 64 + expert_of).astype(F32).astype(BF)
+    col = iota((1, width), 1)
+    slot = (col // (width // PARTS) * SUB + col % SUB).astype(F32)
+    want[...] = jnp.where(col // SUB % blocks == iota((n, width), 0) // rows_of, slot, -2.0)
 
 
 def kernel(
-    tok, cot, routes, probs, wgu, wdn, comb_o, dtok_o, grad_o,
-    s1z, s1x, c1x, a1z, a1x, b1z, b1x, g1, g2, q1, q2, d1, d2, perm, x2, xr, xt, cr, prow,
+    tok, cot, routes, probs, wgu3, wdn, comb_o, dtok_o, grad_o,
+    s1z, s1x, c1x, a1z, a1x, b1z, b1x, g1, g2, q1, q2, d1, d2, wgu, perm, tri, sel1, sel2, want1, want2, x2, xr, xt, cr, prow,
     pa, sb, rb, pb, pq, pr, da, tb, ub, vb, vq, vr, pre, hg, dg, y2, o1, o2, e1, e2, f1, f2, k1, k2,
     ss_a, rs_a, ss_d, rs_d, ss_c, rs_c, ss_q, rs_q, ss_p, rs_p, ss_g, rs_g, ss_w, rs_w, ss_e, rs_e, ss_k, rs_k,
 ):
@@ -101,21 +96,33 @@
 
     relays = ((2, 4, 1), (-2, -4, 2), (1, 3, 0), (-1, -3, 0))
 
+    turn = (4, 3, -3, 2, -2, 1, -1)
+
     def near(d):
         return (y + d) % ny
 
-    def reduce_first(i, value, out, land):
+    def reduce_first(i, value, out, land, final):
+        if i in DIRECT:
+            for d in turn:
+                p = near(d)
+                out[p] = value(p).astype(BF)
+                remote(out.at[p], final.at[y], ss_p.at[i, p], rs_p.at[i, y], at(y_=p)).start()
+            return
         for j, (d, far, cut) in enumerate(relays):
             out[j] = value(near(far)).astype(BF)
             at_ = lanes(out, cut)
             remote(out.at[j, :, at_], land.at[j, :, at_], ss_q.at[i, j], rs_q.at[i, j], at(y_=near(d))).start()
 
     def reduce_next(i, value, out, final):
+        if i in DIRECT:
+            return
         for j, d in ((0, 1), (1, -1)):
             out[4 + j] = value(near(d)).astype(BF)
             remote(out.at[4 + j], final.at[j], ss_p.at[i, j], rs_p.at[i, j], at(y_=near(d))).start()
 
     def reduce_relay(i, value, out, land, final):
+        if i in DIRECT:
+            return
         for j, d in ((2, 2), (3, -2)):
             part, whole = j - 2, j
             cut = lanes(land, j - 1)
@@ -130,12 +137,17 @@
             remote(out.at[4 + j], final.at[j], ss_p.at[i, j], rs_p.at[i, j], at(y_=near(d))).start()
 
     def reduce_done(i, total, final):
-        for j in range(4):
+        for j in [near(d) for d in turn[::-1]] if i in DIRECT else range(4):
             remote(final.at[j], final.at[j], rs_p.at[i, j], rs_p.at[i, j], at()).wait_recv()
             total += final[j].astype(F32)
         return total
 
     def reduce_sent(i, out):
+        if i in DIRECT:
+            for d in turn:
+                p = near(d)
+                remote(out.at[p], out.at[p], ss_p.at[i, p], ss_p.at[i, p], at()).wait_send()
+            return
         for j, (_, _, cut) in enumerate(relays):
             ref = out.at[j, :, lanes(out, cut)]
             remote(ref, ref, ss_q.at[i, j], ss_q.at[i, j], at()).wait_send()
@@ -160,10 +172,17 @@
         remote(ref, ref, ss_w.at[i, near(d)], rs_w.at[i, near(d)], at(c_=1 - c)).start()
 
     def gather_first(i, buf):
-        gather_send(i, buf, (0, 1, 2, 3))
+        if i in SPREAD:
+            for d in turn:
+                p = near(d)
+                remote(buf.at[c, y], buf.at[c, y], ss_g.at[i, p], rs_g.at[i, y], at(y_=p)).start()
+        else:
+            gather_send(i, buf, (0, 1, 2, 3))
         pass_on(i, buf, 0)
 
     def gather_relay(i, buf):
+        if i in SPREAD:
+            return
         gather_got(i, buf, 0)
         gather_send(i, buf, (4, 6))
         gather_got(i, buf, 1)
@@ -175,20 +194,30 @@
             pass_on(i, buf, d)
 
     def gather_done(i, buf):
-        for k, d in ((6, -3), (7, 3)):
-            gather_got(i, buf, k)
-            pass_on(i, buf, d)
-        gather_got(i, buf, 4)
-        gather_got(i, buf, 5)
-        pass_on(i, buf, 4)
+        if i in SPREAD:
+            for d in turn[::-1]:
+                ref = buf.at[c, near(d)]
+                remote(ref, ref, rs_g.at[i, near(d)], rs_g.at[i, near(d)], at()).wait_recv()
+                pass_on(i, buf, d)
+        else:
+            for k, d in ((6, -3), (7, 3)):
+                gather_got(i, buf, k)
+                pass_on(i, buf, d)
+            gather_got(i, buf, 4)
+            gather_got(i, buf, 5)
+            pass_on(i, buf, 4)
         for d in (0, -2, 2, -1, 1, -3, 3, 4):
             ref = buf.at[1 - c, near(d)]
             remote(ref, ref, rs_w.at[i, near(d)], rs_w.at[i, near(d)], at()).wait_recv()
 
     def gather_sent(i, buf):
-        for k, (origin, _, cut) in enumerate(hops):
-            ref = buf.at[c, near(origin), :, lanes(buf, cut)]
-            remote(ref, ref, ss_g.at[i, k], ss_g.at[i, k], at()).wait_send()
+        if i in SPREAD:
+            for d in turn:
+                remote(buf.at[c, y], buf.at[c, y], ss_g.at[i, near(d)], ss_g.at[i, near(d)], at()).wait_send()
+        else:
+            for k, (origin, _, cut) in enumerate(hops):
+                ref = buf.at[c, near(origin), :, lanes(buf, cut)]
+                remote(ref, ref, ss_g.at[i, k], ss_g.at[i, k], at()).wait_send()
         for d in range(ny):
             ref = buf.at[c, near(d)]
             remote(ref, ref, ss_w.at[i, near(d)], ss_w.at[i, near(d)], at()).wait_send()
@@ -241,8 +270,17 @@
         (r_ // SUB // nz == c_ // SUB % nx) & (r_ // SUB % nz == c_ // SUB // nx) & (r_ % SUB == c_ % SUB)
     ).astype(F32).astype(BF)
 
+    wgu[...] = wgu3[...].reshape(span, 2 * hid)
     wide = (1, PARTS * rows)
     dest = iota(wide, 1) % rows
+    r_, c_ = iota(tri.shape, 0), iota(tri.shape, 1)
+    tri[...] = ((r_ // rows_of == c_ // rows_of) & (c_ < r_)).astype(F32).astype(BF)
+    place_plan(z * (nx // 2) + dest // (nz * SUB) // 2, nz, rows_of, sel1, want1)
+    place_plan(dest // (nx * SUB) * (nx // 2) + x // 2, nx, rows_of, sel2, want2)
+
+    def placed(meta, sel, want):
+        return (dot(rank_table(meta, tri[...]), sel[...]) == want[...]).astype(F32).astype(BF)
+
 
     def pack(g, block, q):
         q[...] = dot_tn(g[...], block).astype(BF).reshape(q.shape)
@@ -257,14 +295,12 @@
 
     got(lambda p: a1z.at[p], rs_a.at[0], z, nbz, nz)
     block = a1z[...].reshape(nz * rows_of, 384)
-    table = rank_table(block[:, 256:384].astype(F32), rows_of)
-    g1[...] = place_table(table, z * (nx // 2) + dest // (nz * SUB) // 2, nz, rows_of)
+    g1[...] = placed(block[:, 256:384].astype(F32), sel1, want1)
     pack(g1, block[:, 0:256], q1.at[0])
     slots_x(0, 0)
     got(lambda p: a1x.at[p], rs_a.at[1], x, nbx, nx)
     block = a1x[...].reshape(nx * rows_of, 256)
-    table = rank_table(block[:, 128:256].astype(F32) * (iota((nx * rows_of, 128), 1) >= 64), rows_of)
-    g2[...] = place_table(table, dest // (nx * SUB) * (nx // 2) + x // 2, nx, rows_of)
+    g2[...] = placed(jnp.where(iota((nx * rows_of, 128), 1) >= 64, block[:, 128:256].astype(F32), 0.0), sel2, want2)
     pack(g2, block, q2.at[0])
     slots_z(0, 0)
     slots_x(0, 1)
@@ -277,13 +313,6 @@
         slots_x(1, h)
         slots_z(1, h)
 
-    def sweep(n, body):
-        def step(i, _):
-            body(pl.ds(pl.multiple_of(i * tile, tile), tile), i * tile)
-            return 0
-
-        lax.fori_loop(0, n // tile, step, 0)
-
     expert = z * (nx // 2) + x // 2
     mine, other = c * half, (1 - c) * half
     y2[:, :, 128:256] = jnp.zeros((PARTS, rows, 128), BF)
@@ -292,46 +321,41 @@
         got(lambda p: d1.at[i, h, p], rs_d.at[0, i, h], x, nbx, nx)
         got(lambda p: d2.at[i, h, p], rs_d.at[1, i, h], z, nbz, nz)
 
-    def parts_of(src, weights, near_, far_, back_, i):
-        def far_rows(at_, k):
-            far_[at_, :] = dot(src[pl.ds(pl.multiple_of(other + k, tile), tile), :], weights[...]).astype(BF)
-
-        def near_rows(at_, k):
-            near_[at_, :] = dot(src[pl.ds(pl.multiple_of(mine + k, tile), tile), :], weights[...])
-
-        sweep(half, far_rows)
+    def parts_of(arrange, src, weights, near_, far_, back_, i):
+        at_ = pl.ds(pl.multiple_of(other, half), half)
+        arrange(at_)
+        far_[...] = dot(src[at_, :], weights[...]).astype(BF)
         remote(far_, back_, ss_c.at[i], rs_c.at[i], at(c_=1 - c)).start()
-        sweep(half, near_rows)
+        at_ = pl.ds(pl.multiple_of(mine, half), half)
+        arrange(at_)
+        near_[...] = dot(src[at_, :], weights[...])
 
     def tokens_in(h):
         slots_got(0, h)
-        x2[...] = d2[0, h].reshape(rows, 256)
         xr[h, :, 0:256] = d1[0, h].reshape(rows, 256)
 
-        def arrange(at_, _):
-            lower = dot(perm[at_, :], x2[...])
-            gate = lower[:, 128:256]
-            which = iota((tile, 128), 1)
-            gate = jnp.where((which == 64 + expert) | (which == 96 + expert), gate, 0.0)
-            prow[h, at_, :] = jnp.broadcast_to(jnp.sum(gate, axis=1, keepdims=True), (tile, 128))
-            xr[h, at_, 256:span] = lower[:, 0:tail].astype(BF)
-
-        sweep(rows, arrange)
-        parts_of(xr.at[h], wgu, pa.at[h], sb.at[h], rb.at[h], h)
+        def arrange(at_):
+            xr[h, at_, 256:span] = dot(perm[at_, :], d2[0, h].reshape(rows, 256))[:, 0:tail].astype(BF)
+
+        parts_of(arrange, xr.at[h], wgu, pa.at[h], sb.at[h], rb.at[h], h)
+
+    def gains(h):
+        gate = dot(perm[...], d2[0, h].reshape(rows, 256)[:, 128:256])
+        which = iota((rows, 128), 1)
+        gate = jnp.where((which == 64 + expert) | (which == 96 + expert), gate, 0.0)
+        prow[h] = jnp.broadcast_to(jnp.sum(gate, axis=1, keepdims=True), (rows, 128))
 
     def grads_in(h):
         slots_got(1, h)
-        x2[...] = d2[1, h].reshape(rows, 256)
-        cr[:, 0:256] = d1[1, h].reshape(rows, 256)
-
-        def scale(at_, _):
-            lower = dot(perm[at_, :], x2[...])
+        x2[...] = d1[1, h].reshape(rows, 256)
+
+        def arrange(at_):
             gain = prow[h, at_, 0:1]
+            cr[at_, 0:256] = (x2[at_, :].astype(F32) * gain).astype(BF)
+            lower = dot(perm[at_, :], d2[1, h].reshape(rows, 256))
             cr[at_, 256:span] = (lower[:, 0:tail] * gain).astype(BF)
-            cr[at_, 0:256] = (cr[at_, 0:256].astype(F32) * gain).astype(BF)
-
-        sweep(rows, scale)
-        parts_of(cr, wdn, da.at[h], tb.at[h], ub.at[h], 2 + h)
+
+        parts_of(arrange, cr, wdn, da.at[h], tb.at[h], ub.at[h], 2 + h)
 
     def pre_sum(h):
         def value(p):
@@ -349,12 +373,12 @@
 
     def pre_first(h):
         remote(rb.at[h], rb.at[h], rs_c.at[h], rs_c.at[h], at()).wait_recv()
-        reduce_first(h, pre_sum(h), pb.at[h], pq.at[h])
+        reduce_first(h, pre_sum(h), pb.at[h], pq.at[h], pr.at[h])
         reduce_next(h, pre_sum(h), pb.at[h], pr.at[h])
 
     def dh_first(h):
         remote(ub.at[h], ub.at[h], rs_c.at[2 + h], rs_c.at[2 + h], at()).wait_recv()
-        reduce_first(2 + h, dh_sum(h), vb.at[h], vq.at[h])
+        reduce_first(2 + h, dh_sum(h), vb.at[h], vq.at[h], vr.at[h])
         reduce_next(2 + h, dh_sum(h), vb.at[h], vr.at[h])
 
     def pre_relay(h):
@@ -416,7 +440,9 @@
         out[:, 256:span] = jnp.sum(k2[i].astype(F32), axis=0)[:, 0:tail].astype(BF)
 
     tokens_in(0)
+    gains(0)
     tokens_in(1)
+    gains(1)
     pre_first(0)
     grads_in(0)
     pre_first(1)
@@ -451,9 +477,7 @@
     def weights(j, _):
         at_ = pl.ds(pl.multiple_of(j * step, step), step)
         value = dot(xt[at_, :], dg[...].reshape(PARTS * rows, 2 * hid))
-        for k in range(2):
-            part = value[:, k * hid : (k + 1) * hid]
-            grad_o[pl.ds(j * (step // 8), step // 8), k] = part.reshape(step // 8, 8, hid).astype(BF)
+        grad_o[at_] = value.reshape(step, 2, hid).astype(BF)
         return 0
 
     lax.fori_loop(0, 4, weights, 0)
@@ -499,12 +523,15 @@
         vm((nz, rows_of, 256), BF), vm((nx, rows_of, 256), BF),
         vm((nz * rows_of, h * rows), BF), vm((nx * rows_of, h * rows), BF),
         along_x, along_z, along_x, along_z,
-        vm((rows, rows), BF), vm((rows, 256), BF), vm((h, rows, span), BF), vm((span, h * rows), BF),
+        vm((span, 2 * hid), BF), vm((rows, rows), BF), vm((nz * rows_of, nz * rows_of), BF),
+        vm((128, h * rows), BF), vm((128, h * rows), BF),
+        vm((nz * rows_of, h * rows), F32), vm((nx * rows_of, h * rows), F32),
+        vm((rows, 256), BF), vm((h, rows, span), BF), vm((span, h * rows), BF),
         vm((rows, span), BF), vm((h, rows, 128), F32),
         vm((h, half, 2 * hid), F32), vm((h, half, 2 * hid), BF), vm((h, half, 2 * hid), BF),
-        vm((h, 8, piece, 2 * hid), BF), vm((h, 4, piece, 2 * hid), BF), vm((h, 4, piece, 2 * hid), BF),
+        vm((h, 8, piece, 2 * hid), BF), vm((h, 4, piece, 2 * hid), BF), vm((h, 8, piece, 2 * hid), BF),
         vm((h, half, hid), F32), vm((h, half, hid), BF), vm((h, half, hid), BF),
-        vm((h, 8, piece, hid), BF), vm((h, 4, piece, hid), BF), vm((h, 4, piece, hid), BF),
+        vm((h, 8, piece, hid), BF), vm((h, 4, piece, hid), BF), vm((h, 8, piece, hid), BF),
         vm((h, piece, 2 * hid), F32),
         vm((h, 2, ny, piece, hid), BF), vm((h, 2, ny, piece, 2 * hid), BF),
         vm((h, rows, 256), BF),
@@ -512,7 +539,7 @@
         vm((2, nz, rows_of, 256), BF), vm((2, nx, rows_of, 256), BF),
         vm((2, nz, rows_of, 256), BF), vm((2, nx, rows_of, 256), BF),
         dma((4, n)), dma((4, n)), dma((2, 2, h, n)), dma((2, 2, h, n)), dma((2 * h,)), dma((2 * h,)),
-        dma((2 * h, 4)), dma((2 * h, 4)), dma((2 * h, 4)), dma((2 * h, 4)),
+        dma((2 * h, 4)), dma((2 * h, 4)), dma((2 * h, 8)), dma((2 * h, 8)),
         dma((2 * h, 8)), dma((2 * h, 8)), dma((2 * h, n)), dma((2 * h, n)),
         dma((2, 2, h, n)), dma((2, 2, h, n)), dma((2, 2, n)), dma((2, 2, n)),
     ]
@@ -521,7 +548,7 @@
         out_shape=(
             jax.ShapeDtypeStruct((rows_of, span), BF),
             jax.ShapeDtypeStruct((rows_of, span), BF),
-            jax.ShapeDtypeStruct((span // 8, 2, 8, hid), BF),
+            jax.ShapeDtypeStruct((span, 2, hid), BF),
         ),
         in_specs=[pl.BlockSpec(memory_space=pltpu.VMEM)] * 6,
         out_specs=[pl.BlockSpec(memory_space=pltpu.VMEM)] * 3,
@@ -530,8 +557,8 @@
             collective_id=0, has_side_effects=True, vmem_limit_bytes=48 * 2**20
         ),
         name="expert_layer",
-    )(tokens, cotangent, routes.T, probs.T, w_gate_up.reshape(span, 2 * hid), w_down[0].T)
-    return combined, d_tokens, grad.transpose(0, 2, 1, 3).reshape(1, span, 2, hid)
+    )(tokens, cotangent, routes.T, probs.T, w_gate_up[0], w_down[0].T)
+    return combined, d_tokens, grad[None]
 
 
 def solution(mesh):

time: 89.8 us -> 92.6 us (1.031)
  local copies, waits for them, and re-layouts: 4.58 us -> 7.13 us
    unnamed x14 -> x15, local copies, waits for them, and re-layouts: 4.51 us -> 7.13 us
where the time goes in v3:
time: 92.6 us; the launch traced here: 92.2 us
  Pallas kernels  84.4 us (91%)
  local copies, waits for them, and re-layouts  7.13 us (8%)
    pallas_call x1, Pallas kernels, shards(): pl.pallas_call(kernel, out_shape=(jax.ShapeDtypeStruct((rows_of, span), B...  84.4 us
    unnamed x15, local copies, waits for them, and re-layouts  7.13 us

profile of v3, /device:TPU:1, one launch (start us, length us, event | category | flops | bytes accessed | tf_op | source)
XLA Modules:
  0.0 92.2 jit_solution(4280418367789101481)
XLA Ops:
  0.6 0.0 copy-start.4
  0.6 0.7 copy-done.4
  1.3 0.0 copy-start
  1.3 1.2 %copy-done = bf16[1,448,2,512]{3,2,1,0:T(2,128)(2,1)S(1)} copy-done((bf16[1,448,2,512]{3,2,1,0:T(2,128)(2,1)S(1)}, bf16[1,448,2,512]{3,2,1,0:T(2,128)(2,1)}, u32[]{:S(2)}) %copy-start) | copy-done | bytes 917528
  2.5 0.0 copy-start.1
  2.5 1.0 %copy-done.1 = bf16[1,512,448]{1,2,0:T(8,128)(2,1)S(1)} copy-done((bf16[1,512,448]{1,2,0:T(8,128)(2,1)S(1)}, bf16[1,512,448]{1,2,0:T(8,128)(2,1)}, u32[]{:S(2)}) %copy-start.1) | copy-done | bytes 458776
  3.5 0.0 copy-start.2
  3.5 0.7 copy-done.2
  4.2 0.0 copy-start.3
  4.2 0.7 copy-done.3
  5.0 0.0 copy-start.5
  5.0 0.7 copy-done.5
  5.6 84.4 %expert_layer.1 = (bf16[16,448]{1,0:T(8,128)(2,1)S(1)}, bf16[16,448]{1,0:T(8,128)(2,1)S(1)}, bf16[448,2,512]{2,1,0:T(2,128)(2,1)S(1)}) custom-call(bf16[16,448]{1,0:T(8,128)(2,1)S(1)} %copy-done.2, bf16[16,448]{1,0:T(8,128)(2,1)S(1)} %copy-done.3, s32[8,16]{1,0:T(8,128)S(1)} %bitcast.10, f32[8,16]{1,0:T(8,128)S(1)} %bitcast.11, ...), custom_call_target="tpu_custom_call" | custom-call | tf_op jit(solution)/shard_map/expert_layer/pallas_call | solution.py:546
  90.1 0.6 copy.12
  90.7 0.6 copy.13
  91.3 0.9 copy.14
Async XLA Ops:
  0.6 0.7 copy-start.4
  1.3 1.2 %copy-start = (bf16[1,448,2,512]{3,2,1,0:T(2,128)(2,1)S(1)}, bf16[1,448,2,512]{3,2,1,0:T(2,128)(2,1)}, u32[]{:S(2)}) copy-start(bf16[1,448,2,512]{3,2,1,0:T(2,128)(2,1)} %param.10) | copy-start | bytes 2752516
  2.5 1.0 %copy-start.1 = (bf16[1,512,448]{1,2,0:T(8,128)(2,1)S(1)}, bf16[1,512,448]{1,2,0:T(8,128)(2,1)}, u32[]{:S(2)}) copy-start(bf16[1,512,448]{1,2,0:T(8,128)(2,1)} %param.11) | copy-start | bytes 1376260
  3.5 0.7 copy-start.2
  4.2 0.7 copy-start.3
  5.0 0.7 copy-start.5

commit v4 on v2

--- a/solution.py
+++ b/solution.py
@@ -451,9 +451,7 @@
     def weights(j, _):
         at_ = pl.ds(pl.multiple_of(j * step, step), step)
         value = dot(xt[at_, :], dg[...].reshape(PARTS * rows, 2 * hid))
-        for k in range(2):
-            part = value[:, k * hid : (k + 1) * hid]
-            grad_o[pl.ds(j * (step // 8), step // 8), k] = part.reshape(step // 8, 8, hid).astype(BF)
+        grad_o[at_] = value.reshape(step, 2, hid).astype(BF)
         return 0
 
     lax.fori_loop(0, 4, weights, 0)
@@ -521,7 +519,7 @@
         out_shape=(
             jax.ShapeDtypeStruct((rows_of, span), BF),
             jax.ShapeDtypeStruct((rows_of, span), BF),
-            jax.ShapeDtypeStruct((span // 8, 2, 8, hid), BF),
+            jax.ShapeDtypeStruct((span, 2, hid), BF),
         ),
         in_specs=[pl.BlockSpec(memory_space=pltpu.VMEM)] * 6,
         out_specs=[pl.BlockSpec(memory_space=pltpu.VMEM)] * 3,
@@ -531,7 +529,7 @@
         ),
         name="expert_layer",
     )(tokens, cotangent, routes.T, probs.T, w_gate_up.reshape(span, 2 * hid), w_down[0].T)
-    return combined, d_tokens, grad.transpose(0, 2, 1, 3).reshape(1, span, 2, hid)
+    return combined, d_tokens, grad[None]
 
 
 def solution(mesh):

time: 89.8 us -> 88.8 us (0.989)
  local copies, waits for them, and re-layouts: 4.58 us -> 3.57 us
    unnamed x14, local copies, waits for them, and re-layouts: 4.51 us -> 3.57 us
where the time goes in v4:
time: 88.8 us; the launch traced here: 88.6 us
  Pallas kernels  84.3 us (95%)
  local copies, waits for them, and re-layouts  3.57 us (4%)
    pallas_call x1, Pallas kernels, shards(): pl.pallas_call(kernel, out_shape=(jax.ShapeDtypeStruct((rows_of, span), B...  84.3 us
    unnamed x14, local copies, waits for them, and re-layouts  3.57 us

profile of v4, /device:TPU:1, one launch (start us, length us, event | category | flops | bytes accessed | tf_op | source)
XLA Modules:
  0.0 88.6 jit_solution(7499603368872525123)
XLA Ops:
  0.6 0.0 copy-start
  0.6 0.0 copy-start.1
  0.7 0.0 copy-start.2
  0.7 0.0 copy-start.3
  0.7 0.0 copy-start.4
  0.7 1.4 %copy.9 = bf16[56,8,2,512]{3,1,2,0:T(8,128)(2,1)S(1)} copy(bf16[56,8,2,512]{3,2,1,0:T(2,128)(2,1)} %bitcast.14) | data formatting | bytes 1835008
  2.1 0.0 copy-done
  2.1 0.0 copy-done.1
  2.1 0.0 copy-done.2
  2.1 0.0 copy-done.3
  2.1 0.0 copy-done.4
  2.2 84.3 %expert_layer.1 = (bf16[16,448]{1,0:T(8,128)(2,1)S(1)}, bf16[16,448]{1,0:T(8,128)(2,1)S(1)}, bf16[448,2,512]{2,1,0:T(2,128)(2,1)S(1)}) custom-call(bf16[16,448]{1,0:T(8,128)(2,1)S(1)} %copy-done.1, bf16[16,448]{1,0:T(8,128)(2,1)S(1)} %copy-done.2, s32[8,16]{1,0:T(8,128)S(1)} %bitcast.12, f32[8,16]{1,0:T(8,128)S(1)} %bitcast.13, ...), custom_call_target="tpu_custom_call" | custom-call | tf_op jit(solution)/shard_map/expert_layer/pallas_call | solution.py:517
  86.5 0.6 copy.13
  87.1 0.6 copy.14
  87.7 0.9 %copy.15 = bf16[1,448,2,512]{3,2,1,0:T(2,128)(2,1)} copy(bf16[1,448,2,512]{3,2,1,0:T(2,128)(2,1)S(1)} %bitcast.10) | data formatting | bytes 1835008
Async XLA Ops:
  0.6 1.5 %copy-start = (bf16[1,512,448]{1,2,0:T(8,128)(2,1)S(1)}, bf16[1,512,448]{1,2,0:T(8,128)(2,1)}, u32[]{:S(2)}) copy-start(bf16[1,512,448]{1,2,0:T(8,128)(2,1)} %param.11) | copy-start | bytes 1376260
  0.6 1.5 %copy-start.1 = (bf16[16,448]{1,0:T(8,128)(2,1)S(1)}, bf16[16,448]{1,0:T(8,128)(2,1)}, u32[]{:S(2)}) copy-start(bf16[16,448]{1,0:T(8,128)(2,1)} %tok.1) | copy-start | bytes 43012
  0.7 1.5 %copy-start.2 = (bf16[16,448]{1,0:T(8,128)(2,1)S(1)}, bf16[16,448]{1,0:T(8,128)(2,1)}, u32[]{:S(2)}) copy-start(bf16[16,448]{1,0:T(8,128)(2,1)} %cot.1) | copy-start | bytes 43012
  0.7 1.5 %copy-start.3 = (s32[16,8]{0,1:T(8,128)S(1)}, s32[16,8]{0,1:T(8,128)}, u32[]{:S(2)}) copy-start(s32[16,8]{0,1:T(8,128)} %param.7) | copy-start | bytes 1540
  0.7 1.5 %copy-start.4 = (f32[16,8]{0,1:T(8,128)S(1)}, f32[16,8]{0,1:T(8,128)}, u32[]{:S(2)}) copy-start(f32[16,8]{0,1:T(8,128)} %param.8) | copy-start | bytes 1540
